TPU v7x, 256 devices: a whole 4x4x8 slice. The times are simulated.
256 devices in a mesh: seq: 4 (over z_hi, core), res: 64 (over x, y, z_lo).
Axes of the slice: x: 4, y: 4, z: 8 (z_hi: 2, z_lo: 4; z = z_hi * 4 + z_lo), core: 2. Of those that a mesh axis runs over, the one named last changes fastest.
Arguments:
- homolog_activations: bfloat16 [1024, 768, 64], P('seq', 'res'), may hold values from -6 to 6
- present_entry_flags: int32 [1024, 768], P('seq', 'res'), may hold values from 0 to 1
- normalizer_scale: float32 [64], replicated, may hold values from 0.5 to 1.5
- normalizer_shift: float32 [64], replicated, may hold values from -1.5 to 1.5
- first_factor_weights: bfloat16 [64, 32], replicated, may hold values from -0.75 to 0.75
- first_factor_offset: float32 [32], replicated, may hold values from -0.9 to 0.9
- second_factor_weights: bfloat16 [64, 32], replicated, may hold values from -0.75 to 0.75
- second_factor_offset: float32 [32], replicated, may hold values from -0.9 to 0.9
- pairwise_readout_weights: bfloat16 [1024, 128], replicated, may hold values from -3 to 3
- pairwise_features: bfloat16 [768, 768, 128], P('res', 'seq'), may hold values from -3 to 3
Outputs:
- pair_out: bfloat16 [768, 768, 128], P('res', 'seq')
All inputs are finite; a program needn't handle non-finite values.
Results may differ from a plain program's by a relative error of at most 0.0047.
Values may be sent and summed in bfloat16 or wider, within the bound.
A program may use at most 192 MiB of HBM per device.

v0:
```python
import jax
import jax.numpy as jnp
from jax import lax
from jax.sharding import PartitionSpec as P


def paired_factors(
    homolog_activations,
    present_entry_flags,
    normalizer_scale,
    normalizer_shift,
    first_factor_weights,
    first_factor_offset,
    second_factor_weights,
    second_factor_offset,
):
    standardized_features = homolog_activations.astype(jnp.float32)
    center = jnp.mean(standardized_features, axis=-1, keepdims=True)
    spread = jnp.mean((standardized_features - center) ** 2, axis=-1, keepdims=True)
    normed = (
        (standardized_features - center) * lax.rsqrt(spread + 1e-05) * normalizer_scale
        + normalizer_shift
    ).astype(jnp.bfloat16)
    flat = normed.reshape(-1, normed.shape[-1])
    masked_input = present_entry_flags.astype(jnp.float32)[..., None]
    first_factor_features = jnp.dot(
        flat, first_factor_weights, preferred_element_type=jnp.float32
    ).reshape(normed.shape[:-1] + (-1,))
    second_factor_features = jnp.dot(
        flat, second_factor_weights, preferred_element_type=jnp.float32
    ).reshape(normed.shape[:-1] + (-1,))
    first_factor_features = ((first_factor_features + first_factor_offset) * masked_input).astype(
        jnp.bfloat16
    )
    second_factor_features = (
        (second_factor_features + second_factor_offset) * masked_input
    ).astype(jnp.bfloat16)
    return (first_factor_features, second_factor_features)


def outer_block(left_side, sequence_row_mask, right_side, col_mask, weight_wide):
    seqs, rows, width = left_side.shape
    cols = right_side.shape[1]
    outer = lax.dot_general(
        left_side.reshape(seqs, rows * width),
        right_side.reshape(seqs, cols * width),
        (((0,), (0,)), ((), ())),
        preferred_element_type=jnp.float32,
    )
    outer = (
        outer.reshape(rows, width, cols, width)
        .transpose(0, 2, 1, 3)
        .reshape(rows * cols, width * width)
    )
    projected = jnp.dot(outer, weight_wide, precision=lax.Precision.HIGH).reshape(rows, cols, -1)
    count = lax.dot_general(
        sequence_row_mask, col_mask, (((0,), (0,)), ((), ())), preferred_element_type=jnp.float32
    )
    return (projected, count)


def body(
    homolog_activations,
    present_entry_flags,
    normalizer_scale,
    normalizer_shift,
    first_factor_weights,
    first_factor_offset,
    second_factor_weights,
    second_factor_offset,
    pairwise_readout_weights,
    pairwise_features,
):
    first_factor_features, second_factor_features = paired_factors(
        homolog_activations,
        present_entry_flags,
        normalizer_scale,
        normalizer_shift,
        first_factor_weights,
        first_factor_offset,
        second_factor_weights,
        second_factor_offset,
    )
    weight_wide = pairwise_readout_weights.astype(jnp.float32)
    sequence_row_mask = present_entry_flags.astype(jnp.bfloat16)
    projected, count = outer_block(
        first_factor_features,
        sequence_row_mask,
        lax.all_gather(second_factor_features, "res", axis=1, tiled=True),
        lax.all_gather(sequence_row_mask, "res", axis=1, tiled=True),
        weight_wide,
    )
    summed = projected
    counted = count
    projected, count = (
        lax.psum_scatter(summed, "seq", scatter_dimension=1, tiled=True),
        lax.psum_scatter(counted, "seq", scatter_dimension=1, tiled=True),
    )
    update = projected / (0.001 + count)[..., None]
    return (pairwise_features.astype(jnp.float32) + update).astype(jnp.bfloat16)


def solution(mesh):
    in_specs = (
        P("seq", "res", None),
        P("seq", "res"),
        P(),
        P(),
        P(),
        P(),
        P(),
        P(),
        P(),
        P("res", "seq", None),
    )
    out_specs = P("res", "seq", None)
    return jax.shard_map(body, mesh=mesh, in_specs=in_specs, out_specs=out_specs, check_vma=False)
```

profile of v0, /device:TPU:6, one launch (start us, length us, event | category | flops | bytes accessed | tf_op | source)
XLA Modules:
  0.0 592.6 jit_solution(5385698886078907579)
XLA Ops:
  7.4 0.0 copy-start
  7.4 0.0 all-gather.3.cloned.1.call-start
  7.4 1.1 convert_reduce_fusion
  8.5 1.1 fusion.9
  9.6 0.8 convert_bitcast_fusion
  10.4 2.0 fusion.4
  12.4 0.0 all-gather.3.cloned.1.call-update
  12.4 0.0 reduce-scatter.7.cloned.1.call-start
  12.5 173.5 %all-gather = bf16[64,12,256]{2,1,0:T(8,128)(2,1)S(1)} all-gather(bf16[1,12,256]{2,1,0:T(8,128)(2,1)S(1)} %get-tuple-element.5), channel_id=1, replica_groups=mesh['seq'=4,'res'=64] {'res'}, dimensions={0}, use_global_device_ids=true | all-gather | bytes 399360 | tf_op jit(solution)/shard_map/all_gather | solution.py:90
  186.0 0.1 reshape.41
  186.1 1.7 convolution_bitcast_fusion.1
  187.8 0.0 reduce-scatter.7.cloned.1.call-update
  187.8 0.0 reduce-scatter.5.cloned.1.call-start
  187.8 195.6 %all-gather.3.cloned.1.call-done = bf16[256,768,32]{0,2,1:T(8,128)(2,1)} async-done(((bf16[256,12,32]{0,2,1:T(8,128)(2,1)}), bf16[256,768,32]{0,2,1:T(8,128)(2,1)}) %all-gather.3.cloned.1.call-update) | async-done | bytes 12582928 | tf_op jit(solution)/shard_map/all_gather | solution.py:89
  383.5 21.0 %convolution_bitcast_fusion = f32[12,768,32,32]{1,2,3,0:T(8,128)} fusion(bf16[768,32,256]{2,1,0:T(8,128)(2,1)} %bitcast.44, f32[256,12]{0,1:T(8,128)S(1)} %get-tuple-element.6, f32[32]{0:T(128)} %param.15, bf16[64,32]{0,1:T(8,128)(2,1)} %param.14, bf16[256,12,64]{0,2,1:T(8,128)(2,1)} %param.10, f32[64]{0:T(128)} %param.13, f32[64]{0:T(128)} %param.12, ...), kind=kOutput, calls=%fused_computation | convolution fusion | flops 4845895680 | bytes 50766464 | tf_op jit(solution)/shard_map/dot_general | solution.py:44
  404.5 35.4 %copy.15 = f32[12,768,32,32]{1,3,2,0:T(8,128)} copy(f32[12,768,32,32]{1,2,3,0:T(8,128)} %convolution_bitcast_fusion) | data formatting | bytes 75497472 | tf_op jit(solution)/shard_map/transpose | solution.py:52
  439.9 0.0 copy-done
  439.9 26.3 %fusion.13 = f32[12,768,128]{2,1,0:T(8,128)} fusion(f32[12,768,1024]{1,2,0:T(8,128)} %bitcast.42, bf16[1024,128]{1,0:T(8,128)(2,1)S(1)} %copy-done), kind=kOutput, calls=%fused_computation.20 | convolution fusion | flops 7247757312 | bytes 42729472 | tf_op jit(solution)/shard_map/dot_general | solution.py:55
  466.1 0.0 reduce-scatter.5.cloned.1.call-update
  466.2 0.0 reduce-scatter.7.cloned.1.call-done
  466.2 1.0 copy.20
  467.2 115.5 %reduce-scatter.5.cloned.1.call-done = f32[12,192,128]{2,1,0:T(8,128)} async-done(((f32[12,768,128]{2,1,0:T(8,128)}), f32[12,192,128]{2,1,0:T(8,128)}) %reduce-scatter.5.cloned.1.call-update) | async-done | bytes 1179664 | tf_op jit(solution)/shard_map/reduce_scatter | solution.py:96
  582.7 0.0 copy-done.1
  582.7 2.5 add_convert_fusion
  (4 shorter events, 0.0 us)
Async XLA Ops:
  7.4 432.5 %copy-start = (bf16[1024,128]{1,0:T(8,128)(2,1)S(1)}, bf16[1024,128]{1,0:T(8,128)(2,1)}, u32[]{:S(2)}) copy-start(bf16[1024,128]{1,0:T(8,128)(2,1)} %param.18) | copy-start | bytes 786436
  7.4 376.1 %all-gather.3.cloned.1.call-start = ((), (), s32[]{:S(2)}) async-start(), calls=%async_computation.2 | async-start | bytes 12779520 | tf_op jit(solution)/shard_map/all_gather | solution.py:89
  12.4 453.8 %reduce-scatter.7.cloned.1.call-start = ((), (), s32[]{:S(2)}) async-start(), calls=%async_computation.4 | async-start | bytes 491520
  187.8 394.9 %reduce-scatter.5.cloned.1.call-start = ((), (), s32[]{:S(2)}) async-start(), calls=%async_computation.3 | async-start | bytes 5898240 | tf_op jit(solution)/shard_map/reduce_scatter | solution.py:96
  439.9 142.8 %copy-start.1 = (bf16[12,192,128]{2,1,0:T(8,128)(2,1)S(1)}, bf16[12,192,128]{2,1,0:T(8,128)(2,1)}, u32[]{:S(2)}) copy-start(bf16[12,192,128]{2,1,0:T(8,128)(2,1)} %param.19) | copy-start | bytes 1769476
Sparse Core Ops, SparseCore 0:
  12.6 370.8 all-gather.2
Sparse Core Ops, SparseCore 1:
  187.9 52.6 reduce-scatter.6
  466.3 116.4 reduce-scatter.4
where the time goes:
time: 594 us; the launch traced here: 593 us
  waiting for transfers between devices  311 us (52%)
  blocking collectives  173 us (29%)
  matrix products  51 us (9%)
  local copies, waits for them, and re-layouts  36.4 us (6%)
  between operations  14.9 us (3%)
    all_gather x1, waiting for transfers between devices, body(): lax.all_gather(second_factor_features, 'res', axis=1, tiled=True)  196 us
    all_gather x1, blocking collectives, body(): lax.all_gather(sequence_row_mask, 'res', axis=1, tiled=True)  173 us
    reduce_scatter x1, waiting for transfers between devices, body(): lax.psum_scatter(summed, 'seq', scatter_dimension=1, tiled=True)  116 us
    transpose x1, local copies, waits for them, and re-layouts, outer_block(): outer = outer.reshape(rows, width, cols, width).transpose(0, 2, 1, 3).res...  35.4 us
    dot_general x1, matrix products, outer_block(): jnp.dot(outer, weight_wide, precision=lax.Precision.HIGH)  26.3 us
    dot_general x1, matrix products, outer_block(): lax.dot_general(left_side.reshape(seqs, rows * width), right_side.reshape...  21 us
  transfers between devices with their start and end apart: 3, of which 2 were waited for; matrix products, arithmetic and copies ran while one was open for 14% of the time, Pallas kernels for 0%

commit v1 on v0

v1 whole, which is shorter than its diff:
```python
import functools

import jax
import jax.numpy as jnp
from jax import lax
from jax.experimental import pallas as pl
from jax.experimental.pallas import tpu as pltpu
from jax.sharding import PartitionSpec as P

MESH = pl.DeviceIdType.MESH
NT = (((1,), (1,)), ((), ()))

RING_UP, RING_DOWN = 0, 4
FAR, MATE, Y_UP_A, Y_DN_A, Y_UP_B, Y_DN_B, OPP_A, OPP_B = range(8)
CROSS, FLAG_L, FLAG_R = 24, 25, 26
CORE, OUT = 27, 31
N_SEMS = 43


def place(x, y, z, k):
    return ((z // 4) * 2 + k, (x * 4 + y) * 4 + z % 4)


def kernel(
    lin, rin, fin, w2, out, lc, rown, rb, xs, rcs, stage, send_core, got_core, obuf, orecv, ssem, rsem
):
    seq, res = lax.axis_index("seq"), lax.axis_index("res")
    h, k = seq // 2, seq % 2
    x, y, zl = res // 16, (res // 4) % 4, res % 4
    z = h * 4 + zl
    up_z, dn_z = place(x, y, (z + 1) % 8, k), place(x, y, (z + 7) % 8, k)
    anti, sib = place(x, y, (z + 4) % 8, k), place(x, y, z, 1 - k)
    up_y, dn_y = place(x, (y + 1) % 4, z, k), place(x, (y + 3) % 4, z, k)
    odd = x % 2
    mate = place((x + 1 + 2 * odd) % 4, y, z, k)
    far = place((x + 3 + 2 * odd) % 4, y, z, k)
    line = [place(x, y, h * 4 + (zl + d) % 4, k) for d in (1, 2, 3)]
    p = (x - 2 * h + 4) % 4
    source = p < 2
    a = ((p + 1) // 2) % 2
    b = 1 - a

    def copy(src, dst, sem, dev):
        return pltpu.make_async_remote_copy(
            src_ref=src,
            dst_ref=dst,
            send_sem=ssem.at[sem],
            recv_sem=rsem.at[sem],
            device_id=dev,
            device_id_type=MESH,
        )

    def same(ref, sem, dev):
        return copy(ref, ref, sem, dev)

    barrier = pltpu.get_barrier_semaphore()
    partners = [up_z, dn_z, anti, sib, up_y, dn_y, mate, far] + line
    for dev in partners:
        pl.semaphore_signal(barrier, inc=1, device_id=dev, device_id_type=MESH)

    mine = pl.ds(pl.multiple_of(zl * 16, 16), 16)
    lc[h, 0:32, mine, :] = lin[...]
    lc[h, 32, mine, :] = fin[...]
    rown[0:384, :] = rin[...]
    rown[384:400, :] = fin[...]
    pl.semaphore_wait(barrier, len(partners))

    flag_l = copy(fin, lc.at[h, 33, mine, :], FLAG_L, sib)
    flag_r = copy(fin, rown.at[pl.ds(400, 16), :], FLAG_R, sib)
    flag_l.start()
    flag_r.start()
    flag_l.wait()
    flag_r.wait()

    def lslot(zz, lo=0, n=34):
        return lc.at[zz // 4, pl.ds(lo, n), pl.ds(pl.multiple_of((zz % 4) * 16, 16), 16), :]

    def ring(step, zz, up):
        if step == 4:
            part = (0, 17) if up else (17, 17)
        else:
            part = (0, 34)
        sem = (RING_UP if up else RING_DOWN) + step - 1
        return same(lslot(zz, *part), sem, up_z if up else dn_z)

    def rs(n, which, yy):
        return rb.at[n, which, yy % 4]

    def right(n, what, ref, dev):
        return same(ref, 8 + 8 * n + what, dev)

    def far_a(n):
        return right(n, FAR, rs(n, a, y), far)

    def mate_a(n):
        return right(n, MATE, rs(n, a, y), mate)

    def y_copies(n, which):
        ref = rs(n, a if which == 0 else b, y)
        u, d = (Y_UP_A, Y_DN_A) if which == 0 else (Y_UP_B, Y_DN_B)
        return [right(n, u, ref, up_y), right(n, d, ref, dn_y)]

    def opp_a(n):
        return right(n, OPP_A, rs(n, a, y + 3), up_y)

    def opp_b(n):
        return right(n, OPP_B, rs(n, b, y + 1), dn_y)

    def spread_a(n):
        mate_a(n).start()
        for c in y_copies(n, 0):
            c.start()

    def spread_b(n):
        for c in y_copies(n, 1):
            c.start()

    cross = copy(rown, rb.at[1, odd, y], CROSS, anti)

    @pl.when(jnp.logical_not(source))
    def _():
        cross.start()

    @pl.when(source)
    def _():
        rb[0, odd, y] = rown[...]
        far_a(0).start()
        spread_a(0)

    ring(1, z, True).start()
    ring(1, z, False).start()

    @pl.when(jnp.logical_not(source))
    def _():
        right(0, FAR, rs(0, a, y), far).wait_recv()
        spread_a(0)

    right(0, MATE, rs(0, b, y), mate).wait_recv()
    spread_b(0)

    def ring_on(step):
        ring(step, (z + 8 - step) % 8, True).wait_recv()
        ring(step + 1, (z + 8 - step) % 8, True).start()
        ring(step, (z + step) % 8, False).wait_recv()
        ring(step + 1, (z + step) % 8, False).start()

    ring_on(1)

    @pl.when(source)
    def _():
        cross.wait_recv()
        far_a(1).start()
        spread_a(1)

    @pl.when(jnp.logical_not(source))
    def _():
        right(1, FAR, rs(1, a, y), far).wait_recv()
        spread_a(1)

    right(1, MATE, rs(1, b, y), mate).wait_recv()
    spread_b(1)
    ring_on(2)

    for n in range(2):
        right(n, Y_UP_A, rs(n, a, y + 3), up_y).wait_recv()
        opp_a(n).start()
        right(n, Y_DN_B, rs(n, b, y + 1), dn_y).wait_recv()
        opp_b(n).start()
        if n == 0:
            ring_on(3)
    ring(4, (z + 4) % 8, True).wait_recv()
    ring(4, (z + 4) % 8, False).wait_recv()

    low = lax.broadcasted_iota(jnp.int32, (128, 128), 1) < 64

    def block(which, yy, dst):
        def tile(n, carry):
            o = None
            for part in range(2):
                lt = lc[h if part == 0 else 1 - h, pl.ds(n * 4, 4), :, :].reshape(256, 256)
                t = lax.dot_general(
                    rb[part, which, yy, 0:384, :], lt, NT, preferred_element_type=jnp.float32
                )
                o = t if o is None else o + t
            ob = o.astype(jnp.bfloat16).reshape(6, 2, 32, 256)
            for jj in range(2):
                for cl in range(2):
                    rows = pl.ds(pl.multiple_of(n * 64 + cl * 32, 32), 32)
                    xs[:, rows, jj * 128 : jj * 128 + 128] = ob[:, jj, :, cl * 128 : cl * 128 + 128]
            return carry

        lax.fori_loop(0, 8, tile, 0)
        cnt = jnp.zeros((16, 128), jnp.float32)
        for part in range(2):
            for core in range(2):
                lf = lc[h if part == 0 else 1 - h, 32 + core, :, :]
                cnt += lax.dot_general(
                    rb[part, which, yy, 384 + 16 * core : 400 + 16 * core, :],
                    jnp.concatenate([lf, lf], axis=0),
                    NT,
                    preferred_element_type=jnp.float32,
                )
        rcs[...] = 1.0 / (0.001 + cnt)

        def pair(jp, carry):
            q = jnp.dot(w2[...], xs[jp], preferred_element_type=jnp.float32)
            for jj in range(2):
                j = 2 * jp + jj
                c = jnp.where(low, q[:128, jj * 128 : jj * 128 + 128], q[128:, jj * 128 : jj * 128 + 128])
                t = (c * rcs[pl.ds(j, 1), :]).T
                s = t[:64] + t[64:]
                for zi in range(4):
                    dst[pl.ds(zi * 144 + j, 12, stride=12), :] = s[zi * 16 : zi * 16 + 12]
            return carry

        lax.fori_loop(0, 6, pair, 0)

    steps = (0, 3, 1, 2)
    for s, off in enumerate(steps):
        yy = (y + off) % 4
        if off == 3:
            for n in range(2):
                right(n, Y_UP_B, rs(n, b, yy), up_y).wait_recv()
        if off == 1:
            for n in range(2):
                right(n, Y_DN_A, rs(n, a, yy), dn_y).wait_recv()
        if off == 2:
            for n in range(2):
                right(n, OPP_A, rs(n, a, yy), up_y).wait_recv()
                right(n, OPP_B, rs(n, b, yy), dn_y).wait_recv()
        swap = copy(send_core.at[s], got_core.at[s], CORE + s, sib)
        block(1 - k, yy, send_core.at[s])
        swap.start()
        block(k, yy, stage)
        swap.wait_recv()
        obuf[s] = (stage[...] + got_core[s]).astype(jnp.bfloat16).reshape(4, 144, 128)
        for d in range(3):
            zi = (zl + d + 1) % 4
            copy(obuf.at[s, zi], orecv.at[zl, yy], OUT + 3 * s + d, line[d]).start()
        orecv[zl, yy] = obuf[s, zl]

    for s, off in enumerate(steps):
        yy = (y + off) % 4
        for d in range(3):
            zi = (zl + d + 1) % 4
            src = (zl + 3 - d) % 4
            copy(obuf.at[s, zi], orecv.at[src, yy], OUT + 3 * s + d, line[d]).wait()
        copy(send_core.at[s], got_core.at[s], CORE + s, sib).wait_send()
    out[...] = orecv[...]

    for step in range(1, 5):
        ring(step, (z + 9 - step) % 8, True).wait_send()
        ring(step, (z + step - 1) % 8, False).wait_send()
    for n in range(2):
        for c in [mate_a(n)] + y_copies(n, 0) + y_copies(n, 1) + [opp_a(n), opp_b(n)]:
            c.wait_send()

    @pl.when(source)
    def _():
        far_a(0).wait_send()
        far_a(1).wait_send()

    @pl.when(jnp.logical_not(source))
    def _():
        cross.wait_send()


def exchange(lin, rin, fin, w2):
    bf, f32 = jnp.bfloat16, jnp.float32
    vm = pl.BlockSpec(memory_space=pltpu.VMEM)
    return pl.pallas_call(
        kernel,
        out_shape=jax.ShapeDtypeStruct((4, 4, 144, 128), bf),
        in_specs=[vm] * 4,
        out_specs=vm,
        scratch_shapes=[
            pltpu.VMEM((2, 34, 64, 256), bf),
            pltpu.VMEM((416, 256), bf),
            pltpu.VMEM((2, 2, 4, 416, 256), bf),
            pltpu.VMEM((6, 512, 256), bf),
            pltpu.VMEM((16, 128), f32),
            pltpu.VMEM((576, 128), f32),
            pltpu.VMEM((4, 576, 128), f32),
            pltpu.VMEM((4, 576, 128), f32),
            pltpu.VMEM((4, 4, 144, 128), bf),
            pltpu.VMEM((4, 4, 144, 128), bf),
            pltpu.SemaphoreType.DMA((N_SEMS,)),
            pltpu.SemaphoreType.DMA((N_SEMS,)),
        ],
        compiler_params=pltpu.CompilerParams(
            collective_id=0, has_side_effects=True, vmem_limit_bytes=48 * 2**20
        ),
        name="outer_mean",
    )(lin, rin, fin, w2)


def body(msa, flags, scale, shift, w_left, b_left, w_right, b_right, readout, pair):
    f32, bf = jnp.float32, jnp.bfloat16
    v = msa.astype(f32)
    center = jnp.mean(v, axis=-1, keepdims=True)
    spread = jnp.mean((v - center) ** 2, axis=-1, keepdims=True)
    normed = ((v - center) * lax.rsqrt(spread + 1e-05) * scale + shift).astype(bf)
    mask = flags.astype(f32).T
    left = jnp.einsum("sid,dc->cis", normed, w_left, preferred_element_type=f32)
    left = ((left + b_left[:, None, None]) * mask[None]).astype(bf)
    right = jnp.einsum("sid,de->ies", normed, w_right, preferred_element_type=f32)
    right = ((right + b_right[None, :, None]) * mask[:, None, :]).astype(bf)
    lin = jnp.pad(left, ((0, 0), (0, 4), (0, 0)))
    rin = right.reshape(384, 256)
    fin = jnp.pad(mask.astype(bf), ((0, 4), (0, 0)))
    w2 = readout.reshape(16, 2, 32, 128).transpose(1, 3, 0, 2).reshape(256, 512)
    got = exchange(lin, rin, fin, w2)
    update = got.reshape(4, 4, 12, 12, 128).transpose(2, 1, 0, 3, 4).reshape(12, 192, 128)
    return (pair.astype(f32) + update.astype(f32)).astype(bf)


def solution(mesh):
    in_specs = (
        P("seq", "res", None),
        P("seq", "res"),
        P(),
        P(),
        P(),
        P(),
        P(),
        P(),
        P(),
        P("res", "seq", None),
    )
    return jax.shard_map(
        body, mesh=mesh, in_specs=in_specs, out_specs=P("res", "seq", None), check_vma=False
    )
```

time: 594 us -> 101 us (0.17)
  waiting for transfers between devices: 311 us -> 0 us
  blocking collectives: 173 us -> 0 us
  Pallas kernels: 0 us -> 91.8 us
  matrix products: 51 us -> 0.38 us
  local copies, waits for them, and re-layouts: 36.4 us -> 3 us
  between operations: 14.9 us -> 0.2 us
    all_gather x1 -> x0, waiting for transfers between devices: 196 us -> none  [body(): lax.all_gather(second_factor_features, 'res', axis=1, tiled=True)]
    all_gather x1 -> x0, blocking collectives: 173 us -> none  [body(): lax.all_gather(sequence_row_mask, 'res', axis=1, tiled=True)]
    reduce_scatter x1 -> x0, waiting for transfers between devices: 116 us -> none  [body(): lax.psum_scatter(summed, 'seq', scatter_dimension=1, tiled=True)]
    pallas_call x0 -> x1, Pallas kernels: none -> 91.8 us  [exchange(): pl.pallas_call(kernel, out_shape=jax.ShapeDtypeStruct((4, 4, 144, 128), b...]
    dot_general x3 -> x2, matrix products: 49.3 us -> 0.38 us  [the longest x1 0.19 us: body(): jnp.einsum('sid,de->ies', normed, w_right, preferred_element_type=f32)]
    transpose x1 -> x0, local copies, waits for them, and re-layouts: 35.4 us -> none  [outer_block(): outer = outer.reshape(rows, width, cols, width).transpose(0, 2, 1, 3).res...]
  transfers between devices with their start and end apart: 3 -> 0, of which waited for: 2 -> 0; matrix products, arithmetic and copies ran while one was open for 14% -> 0% of each run, Pallas kernels for 0% -> 0%
where the time goes in v1:
time: 101 us; the launch traced here: 99.7 us
  Pallas kernels  91.8 us (91%)
  other arithmetic  4.35 us (4%)
  local copies, waits for them, and re-layouts  3 us (3%)
    pallas_call x1, Pallas kernels, exchange(): pl.pallas_call(kernel, out_shape=jax.ShapeDtypeStruct((4, 4, 144, 128), b...  91.8 us

profile of v1, /device:TPU:6, one launch (start us, length us, event | category | flops | bytes accessed | tf_op | source)
XLA Modules:
  0.0 99.7 jit_solution(18333764273268904203)
XLA Ops:
  0.0 0.0 copy-start
  0.0 0.0 copy-start.5
  0.0 1.1 %convert_reduce_fusion = f32[256,12]{0,1:T(8,128)S(1)} fusion(bf16[256,12,64]{0,2,1:T(8,128)(2,1)} %param.10), kind=kLoop, calls=%fused_computation.6 | loop fusion | flops 390144 | bytes 405504 | tf_op jit(solution)/shard_map/reduce_sum | solution.py:300
  1.2 1.1 %fusion.5 = f32[256,12]{0,1:T(8,128)S(1)} fusion(bf16[256,12,64]{0,2,1:T(8,128)(2,1)} %param.10, f32[256,12]{0,1:T(8,128)S(1)} %broadcast_multiply_fusion), kind=kLoop, calls=%fused_computation.9 | loop fusion | flops 783360 | bytes 417792 | tf_op jit(solution)/shard_map/reduce_sum | solution.py:301
  2.3 0.7 fusion.13
  3.0 1.2 %copy.21 = bf16[16,2,32,128]{3,1,2,0:T(2,128)(2,1)S(1)} copy(bf16[16,2,32,128]{3,2,1,0:T(8,128)(2,1)} %bitcast.39) | data formatting | bytes 524288 | tf_op jit(solution)/shard_map/reshape | solution.py:311
  4.3 0.0 copy-start.3
  4.3 0.1 copy.22.w2
  4.5 0.0 copy-done.1
  4.5 0.0 copy-start.6
  4.5 0.2 fusion.8
  4.7 0.0 copy-done
  4.7 0.0 copy-done.7
  4.7 0.2 fusion.2
  4.9 0.1 copy-done.3
  5.0 0.2 fusion.11
  5.2 0.2 fusion.9
  5.4 91.8 %outer_mean.1 = bf16[4,4,144,128]{3,2,1,0:T(8,128)(2,1)S(1)} custom-call(bf16[32,16,256]{2,1,0:T(8,128)(2,1)S(1)} %pad.8.lin, bf16[384,256]{1,0:T(8,128)(2,1)S(1)} %bitcast.35, bf16[16,256]{1,0:T(8,128)(2,1)S(1)} %pad.9.fin, bf16[256,512]{1,0:T(8,128)(2,1)S(1)} %copy.22.w2), custom_call_target="tpu_custom_call" | custom-call | tf_op jit(solution)/shard_map/outer_mean/pallas_call | solution.py:271
  97.2 0.2 copy.23
  97.4 0.2 copy.24
  97.6 0.0 copy-start.2
  97.7 0.1 reshape.36
  97.8 0.9 copy-done.2
  98.7 1.0 add_convert_fusion
  (11 shorter events, 0.1 us)
Async XLA Ops:
  0.0 4.7 %copy-start = (bf16[64,32]{0,1:T(8,128)(2,1)S(1)}, bf16[64,32]{0,1:T(8,128)(2,1)}, u32[]{:S(2)}) copy-start(bf16[64,32]{0,1:T(8,128)(2,1)} %param.16) | copy-start | bytes 12292
  0.0 4.5 %copy-start.1 = (bf16[256,12,64]{0,2,1:T(8,128)(2,1)S(1)}, bf16[256,12,64]{0,2,1:T(8,128)(2,1)}, u32[]{:S(2)}) copy-start(bf16[256,12,64]{0,2,1:T(8,128)(2,1)} %param.10) | copy-start | bytes 1179652
  0.0 4.5 %copy-start.4 = (f32[64]{0:T(128)S(1)}, f32[64]{0:T(128)}, u32[]{:S(2)}) copy-start(f32[64]{0:T(128)} %param.13) | copy-start | bytes 772
  0.0 4.5 %copy-start.5 = (f32[64]{0:T(128)S(1)}, f32[64]{0:T(128)}, u32[]{:S(2)}) copy-start(f32[64]{0:T(128)} %param.12) | copy-start | bytes 772
  3.0 1.6 %copy-start.7 = (f32[32]{0:T(128)S(1)}, f32[32]{0:T(128)}, u32[]{:S(2)}) copy-start(f32[32]{0:T(128)} %param.17) | copy-start | bytes 388
  4.3 0.7 copy-start.3
  4.5 0.7 copy-start.6
  97.6 1.1 %copy-start.2 = (bf16[12,192,128]{2,1,0:T(8,128)(2,1)S(1)}, bf16[12,192,128]{2,1,0:T(8,128)(2,1)}, u32[]{:S(2)}) copy-start(bf16[12,192,128]{2,1,0:T(8,128)(2,1)} %param.19) | copy-start | bytes 1769476

commit v2 on v1

v2 whole, which is shorter than its diff:
```python
import functools

import jax
import jax.numpy as jnp
from jax import lax
from jax.experimental import pallas as pl
from jax.experimental.pallas import tpu as pltpu
from jax.sharding import PartitionSpec as P

MESH = pl.DeviceIdType.MESH
NT = (((1,), (1,)), ((), ()))
BF, F32 = jnp.bfloat16, jnp.float32

RING_UP, RING_DOWN = 0, 4
FAR, MATE, Y_UP_A, Y_DN_A, Y_UP_B, Y_DN_B, OPP, MATE_OPP = range(8)
CROSS, CORE, COUNT, OUT = 24, 25, 29, 33
N_SEMS = 45
STEPS = (0, 3, 1, 2)
BLOCK = 400


def place(x, y, z, k):
    return ((z // 4) * 2 + k, (x * 4 + y) * 4 + z % 4)


def kernel(
    msa, flags, vecs, w12, readout, out,
    lown, rown, lp, lc, lf, wide, rb, w2, xs, cnt, got_cnt, rcs, stage, send_core, got_core, obuf, orecv,
    ssem, rsem,
):
    seq, res = lax.axis_index("seq"), lax.axis_index("res")
    h, k = seq // 2, seq % 2
    x, y, zl = res // 16, (res // 4) % 4, res % 4
    z = h * 4 + zl
    up_z, dn_z = place(x, y, (z + 1) % 8, k), place(x, y, (z + 7) % 8, k)
    anti, sib = place(x, y, (z + 4) % 8, k), place(x, y, z, 1 - k)
    up_y, dn_y = place(x, (y + 1) % 4, z, k), place(x, (y + 3) % 4, z, k)
    odd = x % 2
    mate = place((x + 1 + 2 * odd) % 4, y, z, k)
    far = place((x + 3 + 2 * odd) % 4, y, z, k)
    line = [place(x, y, h * 4 + (zl + d) % 4, k) for d in (1, 2, 3)]
    p = (x - 2 * h + 4) % 4
    source = p < 2
    a = ((p + 1) // 2) % 2
    b = 1 - a

    def copy(src, dst, sem, dev):
        return pltpu.make_async_remote_copy(
            src_ref=src,
            dst_ref=dst,
            send_sem=ssem.at[sem],
            recv_sem=rsem.at[sem],
            device_id=dev,
            device_id_type=MESH,
        )

    def same(ref, sem, dev):
        return copy(ref, ref, sem, dev)

    barrier = pltpu.get_barrier_semaphore()
    partners = [up_z, dn_z, anti, sib, up_y, dn_y, mate, far] + line
    for dev in partners:
        pl.semaphore_signal(barrier, inc=1, device_id=dev, device_id_type=MESH)

    scale, shift, offset = vecs[:, 0:1], vecs[:, 1:2], vecs[:, 2:3]

    def residue(i, carry):
        v = msa[i].astype(F32)
        c = v - jnp.mean(v, axis=0, keepdims=True)
        var = jnp.mean(c * c, axis=0, keepdims=True)
        normed = (c * lax.rsqrt(var + 1e-05) * scale + shift).astype(BF)
        both = jnp.dot(w12[...], normed, preferred_element_type=F32)
        both = ((both + offset) * flags[pl.ds(i, 1), :].astype(F32)).astype(BF)
        rows = pl.ds(pl.multiple_of(i * 32, 32), 32)
        lown[rows, :] = both[:32]
        rown[rows, :] = both[32:]
        return carry

    lax.fori_loop(0, 12, residue, 0, unroll=6)
    mask = jnp.concatenate([flags[...].astype(F32), jnp.zeros((4, 256), F32)], axis=0).astype(BF)
    lown[384:400, :] = mask
    rown[384:400, :] = mask
    wide[:, 384:512, :] = jnp.zeros((2, 128, 128), F32)
    pl.semaphore_wait(barrier, len(partners))

    def ring(step, zz, up):
        lo, n = (0, BLOCK) if step < 4 else (0, 208) if up else (208, 192)
        sem = (RING_UP if up else RING_DOWN) + step - 1
        dst = lp.at[zz, pl.ds(lo, n), :]
        src = lown.at[pl.ds(lo, n), :] if step == 1 else dst
        return copy(src, dst, sem, up_z if up else dn_z)

    def repack(src, zz):
        part, at = (zz // 4 + h) % 2, pl.ds(pl.multiple_of((zz % 4) * 16, 16), 16)
        for half in range(2):
            lanes = slice(half * 128, half * 128 + 128)
            wide[half, 0:384, :] = src[0:384, lanes].astype(F32)
            for c in range(32):
                lc[part, c, at, lanes] = wide[half, pl.ds(c, 16, stride=32), :].astype(BF)
        lf[part, at, :] = src[384:400, :]

    def ring_on(step, up):
        zz = (z + 8 - step) % 8 if up else (z + step) % 8
        ring(step, zz, up).wait_recv()
        ring(step + 1, zz, up).start()

    def ring_repack(step):
        repack(lp.at[(z + 8 - step) % 8], (z + 8 - step) % 8)
        repack(lp.at[(z + step) % 8], (z + step) % 8)

    def rs(n, which, yy):
        return rb.at[n, which, yy % 4]

    def right(n, what, which, yy, dev):
        return same(rs(n, which, yy), 8 + 8 * n + what, dev)

    def far_a(n):
        return right(n, FAR, a, y, far)

    def mate_a(n):
        return right(n, MATE, a, y, mate)

    def y_copies(n, which):
        u, d = (Y_UP_A, Y_DN_A) if which == 0 else (Y_UP_B, Y_DN_B)
        side = a if which == 0 else b
        return [right(n, u, side, y, up_y), right(n, d, side, y, dn_y)]

    def opp_y(n):
        return right(n, OPP, a, y + 3, up_y) if n == 0 else right(n, OPP, a, y + 1, dn_y)

    def opp_far(n):
        return right(n, OPP, a, y + 2, far)

    def opp_mate(n):
        return right(n, MATE_OPP, a, y + 2, mate)

    def wait(n, what):
        which, yy = {
            FAR: (a, y), MATE: (b, y), Y_UP_A: (a, y + 3), Y_DN_A: (a, y + 1), Y_UP_B: (b, y + 3),
            Y_DN_B: (b, y + 1), OPP: (a, y + 2), MATE_OPP: (b, y + 2),
        }[what]
        right(n, what, which, yy, sib).wait_recv()

    def spread_b(n):
        wait(n, MATE)
        for c in y_copies(n, 1):
            c.start()

    cross = copy(rown, rb.at[1, odd, y], CROSS, anti)

    @pl.when(source)
    def _():
        rb[0, odd, y] = rown[...]
        far_a(0).start()
        mate_a(0).start()
        for c in y_copies(0, 0):
            c.start()
        ring(1, z, True).start()
        ring(1, z, False).start()
        spread_b(0)
        wait(0, Y_UP_A)
        opp_y(0).start()
        ring_on(1, True)
        ring_on(1, False)
        cross.wait_recv()
        far_a(1).start()
        mate_a(1).start()
        for c in y_copies(1, 0):
            c.start()
        wait(0, OPP)
        opp_far(0).start()
        opp_mate(0).start()

    @pl.when(jnp.logical_not(source))
    def _():
        cross.start()
        ring(1, z, True).start()
        ring(1, z, False).start()
        wait(0, FAR)
        mate_a(0).start()
        for c in y_copies(0, 0):
            c.start()
        ring_on(1, True)
        ring_on(1, False)
        spread_b(0)

    repack(lown, z)
    ring_repack(1)
    for cp in range(16):
        w2[:, cp * 32 : cp * 32 + 32] = jnp.concatenate(
            [readout[cp * 64 : cp * 64 + 32, :].T, readout[cp * 64 + 32 : cp * 64 + 64, :].T], axis=0
        )
    ring_on(2, True)
    ring_on(2, False)

    @pl.when(source)
    def _():
        spread_b(1)
        wait(1, Y_DN_A)
        opp_y(1).start()

    @pl.when(jnp.logical_not(source))
    def _():
        wait(1, FAR)
        mate_a(1).start()
        for c in y_copies(1, 0):
            c.start()
        wait(0, OPP)
        opp_mate(0).start()

    ring_repack(2)
    ring_on(3, True)
    ring_on(3, False)

    @pl.when(jnp.logical_not(source))
    def _():
        spread_b(1)

    @pl.when(source)
    def _():
        wait(1, OPP)
        opp_far(1).start()
        opp_mate(1).start()

    ring_repack(3)
    ring(4, (z + 4) % 8, True).wait_recv()
    ring(4, (z + 4) % 8, False).wait_recv()
    repack(lp.at[(z + 4) % 8], (z + 4) % 8)

    low = lax.broadcasted_iota(jnp.int32, (128, 128), 1) < 64

    def counts(s, yy):
        for which in range(2):
            t = jnp.zeros((16, 128), F32)
            for part in range(2):
                two = jnp.concatenate([lf[part], lf[part]], axis=0)
                t += lax.dot_general(
                    rb[part, which, yy, 384:400, :], two, NT, preferred_element_type=F32
                )
            cnt[s, which] = t

    def multiply(which, yy):
        def tile(n, carry):
            o = None
            for part in range(2):
                lt = lc[part, pl.ds(n * 4, 4), :, :].reshape(256, 256)
                t = lax.dot_general(rb[part, which, yy, 0:384, :], lt, NT, preferred_element_type=F32)
                o = t if o is None else o + t
            ob = o.astype(BF).reshape(6, 2, 32, 256)
            for jj in range(2):
                for cl in range(2):
                    rows = pl.ds(pl.multiple_of(n * 64 + cl * 32, 32), 32)
                    xs[:, rows, jj * 128 : jj * 128 + 128] = ob[:, jj, :, cl * 128 : cl * 128 + 128]
            return carry

        lax.fori_loop(0, 8, tile, 0, unroll=True)

    def project(dst):
        def pair(jp, carry):
            q = jnp.dot(w2[...], xs[jp], preferred_element_type=F32)
            for jj in range(2):
                j = 2 * jp + jj
                c = jnp.where(low, q[:128, jj * 128 : jj * 128 + 128], q[128:, jj * 128 : jj * 128 + 128])
                t = (c * rcs[pl.ds(j, 1), :]).T
                s = t[:64] + t[64:]
                for zi in range(4):
                    dst[pl.ds(zi * 144 + j, 12, stride=12), :] = s[zi * 16 : zi * 16 + 12]
            return carry

        lax.fori_loop(0, 6, pair, 0, unroll=True)

    for s, off in enumerate(STEPS):
        yy = (y + off) % 4
        if off == 3:
            for n in range(2):
                if n == 0:

                    @pl.when(jnp.logical_not(source))
                    def _():
                        wait(0, Y_UP_A)
                else:
                    wait(1, Y_UP_A)
                wait(n, Y_UP_B)
        if off == 1:
            for n in range(2):
                if n == 1:

                    @pl.when(jnp.logical_not(source))
                    def _():
                        wait(1, Y_DN_A)
                else:
                    wait(0, Y_DN_A)
                wait(n, Y_DN_B)
        if off == 2:
            for n in range(2):
                wait(n, MATE_OPP)
        swap = copy(send_core.at[s], got_core.at[s], CORE + s, sib)
        counts(s, yy)
        swap_counts = copy(cnt.at[s], got_cnt.at[s], COUNT + s, sib)
        swap_counts.start()
        multiply(1 - k, yy)
        swap_counts.wait()
        rcs[...] = 1.0 / (0.001 + cnt[s, 1 - k] + got_cnt[s, 1 - k])
        project(send_core.at[s])
        swap.start()
        if off == 0:

            @pl.when(jnp.logical_not(source))
            def _():
                wait(1, OPP)
                opp_mate(1).start()

        rcs[...] = 1.0 / (0.001 + cnt[s, k] + got_cnt[s, k])
        multiply(k, yy)
        project(stage)
        swap.wait_recv()
        obuf[s] = (stage[...] + got_core[s]).astype(BF).reshape(4, 144, 128)
        for d in range(3):
            zi = (zl + d + 1) % 4
            copy(obuf.at[s, zi], orecv.at[zl, yy], OUT + 3 * s + d, line[d]).start()
        orecv[zl, yy] = obuf[s, zl]

    for s, off in enumerate(STEPS):
        yy = (y + off) % 4
        for d in range(3):
            zi = (zl + d + 1) % 4
            src = (zl + 3 - d) % 4
            copy(obuf.at[s, zi], orecv.at[src, yy], OUT + 3 * s + d, line[d]).wait()
        copy(send_core.at[s], got_core.at[s], CORE + s, sib).wait_send()
    out[...] = orecv[...]

    for step in range(1, 5):
        ring(step, (z + 9 - step) % 8, True).wait_send()
        ring(step, (z + step - 1) % 8, False).wait_send()
    for n in range(2):
        for c in [mate_a(n), opp_mate(n)] + y_copies(n, 0) + y_copies(n, 1):
            c.wait_send()

    @pl.when(source)
    def _():
        for n in range(2):
            for c in [far_a(n), opp_y(n), opp_far(n)]:
                c.wait_send()

    @pl.when(jnp.logical_not(source))
    def _():
        cross.wait_send()


def exchange(*args):
    vm = pl.BlockSpec(memory_space=pltpu.VMEM)
    return pl.pallas_call(
        kernel,
        out_shape=jax.ShapeDtypeStruct((4, 4, 144, 128), BF),
        in_specs=[vm] * len(args),
        out_specs=vm,
        scratch_shapes=[
            pltpu.VMEM((BLOCK, 256), BF),
            pltpu.VMEM((BLOCK, 256), BF),
            pltpu.VMEM((8, BLOCK, 256), BF),
            pltpu.VMEM((2, 32, 64, 256), BF),
            pltpu.VMEM((2, 64, 256), BF),
            pltpu.VMEM((2, 512, 128), F32),
            pltpu.VMEM((2, 2, 4, BLOCK, 256), BF),
            pltpu.VMEM((256, 512), BF),
            pltpu.VMEM((6, 512, 256), BF),
            pltpu.VMEM((4, 2, 16, 128), F32),
            pltpu.VMEM((4, 2, 16, 128), F32),
            pltpu.VMEM((16, 128), F32),
            pltpu.VMEM((576, 128), F32),
            pltpu.VMEM((4, 576, 128), F32),
            pltpu.VMEM((4, 576, 128), F32),
            pltpu.VMEM((4, 4, 144, 128), BF),
            pltpu.VMEM((4, 4, 144, 128), BF),
            pltpu.SemaphoreType.DMA((N_SEMS,)),
            pltpu.SemaphoreType.DMA((N_SEMS,)),
        ],
        compiler_params=pltpu.CompilerParams(
            collective_id=0, has_side_effects=True, vmem_limit_bytes=48 * 2**20
        ),
        name="outer_mean",
    )(*args)


def body(msa, flags, scale, shift, w_left, b_left, w_right, b_right, readout, pair):
    vecs = jnp.stack([scale, shift, jnp.concatenate([b_left, b_right])], axis=1)
    w12 = jnp.concatenate([w_left.T, w_right.T], axis=0)
    got = exchange(msa.transpose(1, 2, 0), flags.T, vecs, w12, readout)
    update = got.reshape(4, 4, 12, 12, 128).transpose(2, 1, 0, 3, 4).reshape(12, 192, 128)
    return (pair.astype(F32) + update.astype(F32)).astype(BF)


def solution(mesh):
    in_specs = (
        P("seq", "res", None),
        P("seq", "res"),
        P(),
        P(),
        P(),
        P(),
        P(),
        P(),
        P(),
        P("res", "seq", None),
    )
    return jax.shard_map(
        body, mesh=mesh, in_specs=in_specs, out_specs=P("res", "seq", None), check_vma=False
    )
```

time: 101 us -> 68.2 us (0.68)
  Pallas kernels: 91.8 us -> 60.5 us
  local copies, waits for them, and re-layouts: 3 us -> 4.24 us
  other arithmetic: 4.35 us -> 3.11 us
    pallas_call x1, Pallas kernels: 91.8 us -> 60.5 us  [exchange(): pl.pallas_call(kernel, out_shape=jax.ShapeDtypeStruct((4, 4, 144, 128), B...]
    unnamed x17 -> x8, local copies, waits for them, and re-layouts: 1.08 us -> 3.61 us
    reduce_sum x2 -> x0, other arithmetic: 2.25 us -> none  [the longest x1 1.13 us: body(): center = jnp.mean(v, axis=-1, keepdims=True)]
    another operation x0 -> x2, other arithmetic: none -> 1.43 us  [body(): vecs = jnp.stack([scale, shift, jnp.concatenate([b_left, b_right])], axis=1)]
    reshape x2 -> x0, local copies, waits for them, and re-layouts: 1.35 us -> none  [body(): w2 = readout.reshape(16, 2, 32, 128).transpose(1, 3, 0, 2).reshape(256, 512)]
    convert_element_type x4 -> x1, other arithmetic: 2.09 us -> 0.96 us  [body(): return (pair.astype(F32) + update.astype(F32)).astype(BF)]
where the time goes in v2:
time: 68.2 us; the launch traced here: 67.9 us
  Pallas kernels  60.5 us (89%)
  local copies, waits for them, and re-layouts  4.24 us (6%)
  other arithmetic  3.11 us (5%)
    pallas_call x1, Pallas kernels, exchange(): pl.pallas_call(kernel, out_shape=jax.ShapeDtypeStruct((4, 4, 144, 128), B...  60.5 us
    unnamed x8, local copies, waits for them, and re-layouts  3.61 us
    another operation x2, other arithmetic, body(): vecs = jnp.stack([scale, shift, jnp.concatenate([b_left, b_right])], axis=1)  1.43 us

profile of v2, /device:TPU:6, one launch (start us, length us, event | category | flops | bytes accessed | tf_op | source)
XLA Modules:
  0.0 67.9 jit_solution(1683331173927329285)
XLA Ops:
  0.0 0.7 %maximum_bitcast_fusion = f32[64,1]{0,1:T(1,128)S(1)} fusion(f32[32]{0:T(128)} %param.17, f32[32]{0:T(128)} %param.15), kind=kLoop, calls=%fused_computation.3 | loop fusion | flops 64 | bytes 512 | tf_op jit(solution)/shard_map/stack | solution.py:386
  0.7 0.7 %pad_maximum_fusion.1 = f32[64,3]{0,1:T(4,128)S(1)} fusion(f32[64,1]{0,1:T(1,128)S(1)} %maximum_bitcast_fusion, f32[64,1]{0,1:T(1,128)} %bitcast.16, f32[64,1]{0,1:T(1,128)} %bitcast.17), kind=kLoop, calls=%fused_computation.2 | loop fusion | flops 384 | bytes 1536 | tf_op jit(solution)/shard_map/stack | solution.py:386
  1.4 0.7 %pad_maximum_fusion.w12 = bf16[64,64]{1,0:T(8,128)(2,1)S(1)} fusion(bf16[32,64]{1,0:T(8,128)(2,1)} %bitcast.14, bf16[32,64]{1,0:T(8,128)(2,1)} %bitcast.15), kind=kLoop, calls=%fused_computation.1 | loop fusion | flops 16384 | bytes 16384 | tf_op jit(solution)/shard_map/concatenate | solution.py:387
  2.1 0.1 copy.20.vecs
  2.2 0.0 copy-start
  2.2 1.0 %copy-done = bf16[256,12,64]{0,2,1:T(8,128)(2,1)S(1)} copy-done((bf16[256,12,64]{0,2,1:T(8,128)(2,1)S(1)}, bf16[256,12,64]{0,2,1:T(8,128)(2,1)}, u32[]{:S(2)}) %copy-start) | copy-done | bytes 393240
  3.2 0.0 copy-start.1
  3.2 0.9 %copy-done.1 = bf16[1024,128]{1,0:T(8,128)(2,1)S(1)} copy-done((bf16[1024,128]{1,0:T(8,128)(2,1)S(1)}, bf16[1024,128]{1,0:T(8,128)(2,1)}, u32[]{:S(2)}) %copy-start.1) | copy-done | bytes 262168
  4.2 0.0 copy-start.2
  4.2 0.7 %copy-done.2 = s32[256,12]{0,1:T(8,128)S(1)} copy-done((s32[256,12]{0,1:T(8,128)S(1)}, s32[256,12]{0,1:T(8,128)}, u32[]{:S(2)}) %copy-start.2) | copy-done | bytes 12312
  4.9 60.5 %outer_mean.1 = bf16[4,4,144,128]{3,2,1,0:T(8,128)(2,1)S(1)} custom-call(bf16[12,64,256]{2,1,0:T(8,128)(2,1)S(1)} %bitcast.11, s32[12,256]{1,0:T(8,128)S(1)} %bitcast.12, f32[64,3]{1,0:T(8,128)S(1)} %copy.20.vecs, bf16[64,64]{1,0:T(8,128)(2,1)S(1)} %pad_maximum_fusion.w12, bf16[1024,128]{1,0:T(8,128)(2,1)S(1)} %copy-done.1), custom_call_target="tpu_custom_call" | custom-call | tf_op jit(solution)/shard_map/outer_mean/pallas_call | solution.py:352
  65.4 0.2 copy.21
  65.6 0.2 copy.22
  65.8 0.0 copy-start.3
  65.9 0.1 reshape.6
  66.0 0.9 %copy-done.3 = bf16[12,192,128]{2,1,0:T(8,128)(2,1)S(1)} copy-done((bf16[12,192,128]{2,1,0:T(8,128)(2,1)S(1)}, bf16[12,192,128]{2,1,0:T(8,128)(2,1)}, u32[]{:S(2)}) %copy-start.3) | copy-done | bytes 589848
  66.9 1.0 %add_convert_fusion = bf16[12,192,128]{2,1,0:T(8,128)(2,1)} fusion(f32[12,192,128]{2,1,0:T(8,128)S(1)} %reshape.6, bf16[12,192,128]{2,1,0:T(8,128)(2,1)S(1)} %copy-done.3), kind=kLoop, calls=%fused_computation | loop fusion | flops 884736 | bytes 2359296 | tf_op jit(solution)/shard_map/convert_element_type | solution.py:390
Async XLA Ops:
  2.2 1.0 %copy-start = (bf16[256,12,64]{0,2,1:T(8,128)(2,1)S(1)}, bf16[256,12,64]{0,2,1:T(8,128)(2,1)}, u32[]{:S(2)}) copy-start(bf16[256,12,64]{0,2,1:T(8,128)(2,1)} %param.10) | copy-start | bytes 1179652
  3.2 0.9 %copy-start.1 = (bf16[1024,128]{1,0:T(8,128)(2,1)S(1)}, bf16[1024,128]{1,0:T(8,128)(2,1)}, u32[]{:S(2)}) copy-start(bf16[1024,128]{1,0:T(8,128)(2,1)} %readout.1) | copy-start | bytes 786436
  4.2 0.7 %copy-start.2 = (s32[256,12]{0,1:T(8,128)S(1)}, s32[256,12]{0,1:T(8,128)}, u32[]{:S(2)}) copy-start(s32[256,12]{0,1:T(8,128)} %param.11) | copy-start | bytes 36868
  65.8 1.1 %copy-start.3 = (bf16[12,192,128]{2,1,0:T(8,128)(2,1)S(1)}, bf16[12,192,128]{2,1,0:T(8,128)(2,1)}, u32[]{:S(2)}) copy-start(bf16[12,192,128]{2,1,0:T(8,128)(2,1)} %param.19) | copy-start | bytes 1769476

commit v3 on v2

v3 whole, which is shorter than its diff:
```python
import functools

import jax
import jax.numpy as jnp
from jax import lax
from jax.experimental import pallas as pl
from jax.experimental.pallas import tpu as pltpu
from jax.sharding import PartitionSpec as P

MESH = pl.DeviceIdType.MESH
NT = (((1,), (1,)), ((), ()))
BF, F32 = jnp.bfloat16, jnp.float32

RING_UP, RING_DOWN, PLANE = 0, 7, 14
FAR, MATE, Y_UP_A, Y_DN_A, Y_UP_B, Y_DN_B, OPP, MATE_OPP = range(8)
CROSS, CORE, COUNT, OUT = 46, 48, 52, 56
RELAY = 68
N_SEMS = 69
STEPS = (0, 3, 1, 2)
BLOCK = 400
HALVES = ((0, 208), (208, 192))


def place(x, y, z, k):
    return ((z // 4) * 2 + k, (x * 4 + y) * 4 + z % 4)


def kernel(
    msa_in, flags_in, scale_in, shift_in, w_left_in, b_left_in, w_right_in, b_right_in, readout_in, pair, out,
    lown, rown, lp, lc, lf, wide, rb, w2, xs, cnt, got_cnt, rcs, stage, send_core, got_core, obuf, orecv,
    w12, pairs, relay, msa, flags, scale, shift, w_left, b_left, w_right, b_right, readout, ssem, rsem, lsem,
):
    seq, res = lax.axis_index("seq"), lax.axis_index("res")
    h, k = seq // 2, seq % 2
    x, y, zl = res // 16, (res // 4) % 4, res % 4
    z = h * 4 + zl
    up_z, dn_z = place(x, y, (z + 1) % 8, k), place(x, y, (z + 7) % 8, k)
    anti, sib = place(x, y, (z + 4) % 8, k), place(x, y, z, 1 - k)
    up_y, dn_y = place(x, (y + 1) % 4, z, k), place(x, (y + 3) % 4, z, k)
    odd = x % 2
    mate = place((x + 1 + 2 * odd) % 4, y, z, k)
    far = place((x + 3 + 2 * odd) % 4, y, z, k)
    line = [place(x, y, h * 4 + (zl + d) % 4, k) for d in (1, 2, 3)]
    p = (x - 2 * h + 4) % 4
    source = p < 2
    a = ((p + 1) // 2) % 2
    b = 1 - a

    def copy(src, dst, sem, dev):
        return pltpu.make_async_remote_copy(
            src_ref=src,
            dst_ref=dst,
            send_sem=ssem.at[sem],
            recv_sem=rsem.at[sem],
            device_id=dev,
            device_id_type=MESH,
        )

    def same(ref, sem, dev):
        return copy(ref, ref, sem, dev)

    barrier = pltpu.get_barrier_semaphore()
    partners = [up_z, dn_z, anti, sib, up_y, dn_y, mate, far] + line
    for dev in partners:
        pl.semaphore_signal(barrier, inc=1, device_id=dev, device_id_type=MESH)

    loads = [
        pltpu.make_async_copy(src, dst, lsem.at[i])
        for i, (src, dst) in enumerate((
            (msa_in, msa), (flags_in, flags), (scale_in, scale), (shift_in, shift), (w_left_in, w_left),
            (b_left_in, b_left), (w_right_in, w_right), (b_right_in, b_right), (readout_in, readout), (pair, pairs),
        ))
    ]
    for load in loads:
        load.start()
    for load in loads[:8]:
        load.wait()
    w12[0:32, :] = w_left[...]
    w12[32:64, :] = w_right[...]

    def column(row):
        square = (row.shape[1], row.shape[1])
        diagonal = lax.broadcasted_iota(jnp.int32, square, 0) == lax.broadcasted_iota(jnp.int32, square, 1)
        return jnp.sum(jnp.where(diagonal, row, 0.0), axis=1, keepdims=True)

    gain, bias = column(scale[...]), column(shift[...])
    offset = jnp.concatenate([column(b_left[...]), column(b_right[...])], axis=0)

    def residue(i, carry):
        v = msa[i].astype(F32)
        c = v - jnp.mean(v, axis=0, keepdims=True)
        var = jnp.mean(c * c, axis=0, keepdims=True)
        normed = (c * lax.rsqrt(var + 1e-05) * gain + bias).astype(BF)
        both = jnp.dot(w12[...], normed, preferred_element_type=F32)
        both = ((both + offset) * flags[pl.ds(i, 1), :].astype(F32)).astype(BF)
        rows = pl.ds(pl.multiple_of(i * 32, 32), 32)
        lown[rows, :] = both[:32]
        rown[rows, :] = both[32:]
        return carry

    lax.fori_loop(0, 12, residue, 0, unroll=6)
    mask = jnp.concatenate([flags[...].astype(F32), jnp.zeros((4, 256), F32)], axis=0).astype(BF)
    lown[384:400, :] = mask
    rown[384:400, :] = mask
    wide[:, 384:512, :] = jnp.zeros((2, 128, 128), F32)
    pl.semaphore_wait(barrier, len(partners))

    def ring(step, zz, up, c):
        sem = (RING_UP if up else RING_DOWN) + 2 * (step - 1) + (c if step < 4 else 0)
        dst = lp.at[zz, pl.ds(*HALVES[c]), :]
        src = lown.at[pl.ds(*HALVES[c]), :] if step == 1 else dst
        return copy(src, dst, sem, up_z if up else dn_z)

    def ring_pieces(step):
        return [(up, c) for c in range(2) for up in (True, False) if step < 4 or up == (c == 0)]

    def ring_from(step, up):
        return (z + 8 - step) % 8 if up else (z + step) % 8

    def ring_on(step, c):
        for up in (True, False):
            ring(step, ring_from(step, up), up, c).wait_recv()
            if (up, c) in ring_pieces(step + 1):
                ring(step + 1, ring_from(step, up), up, c).start()

    def repack(src, zz):
        part, at = (zz // 4 + h) % 2, pl.ds(pl.multiple_of((zz % 4) * 16, 16), 16)
        for half in range(2):
            lanes = slice(half * 128, half * 128 + 128)
            wide[half, 0:384, :] = src[0:384, lanes].astype(F32)
            for c in range(32):
                lc[part, c, at, lanes] = wide[half, pl.ds(c, 16, stride=32), :].astype(BF)
        lf[part, at, :] = src[384:400, :]

    def ring_repack(step):
        repack(lp.at[(z + 8 - step) % 8], (z + 8 - step) % 8)
        repack(lp.at[(z + step) % 8], (z + step) % 8)

    def right(n, what, which, yy, dev, c):
        ref = rb.at[n, which, yy % 4, pl.ds(*HALVES[c]), :]
        return same(ref, PLANE + 2 * (8 * n + what) + c, dev)

    def far_a(n, c):
        return right(n, FAR, a, y, far, c)

    def mate_a(n, c):
        return right(n, MATE, a, y, mate, c)

    def y_copies(n, which, c):
        u, d = (Y_UP_A, Y_DN_A) if which == 0 else (Y_UP_B, Y_DN_B)
        side = a if which == 0 else b
        return [right(n, u, side, y, up_y, c), right(n, d, side, y, dn_y, c)]

    def opp_y(n, c):
        if n == 0:
            return right(n, OPP, a, y + 3, up_y, c)
        return right(n, OPP, a, y + 1, dn_y, c)

    def opp_far(n, c):
        return right(n, OPP, a, y + 2, far, c)

    def opp_mate(n, c):
        return right(n, MATE_OPP, a, y + 2, mate, c)

    def wait(n, what, c):
        which, yy = {
            FAR: (a, y), MATE: (b, y), Y_UP_A: (a, y + 3), Y_DN_A: (a, y + 1), Y_UP_B: (b, y + 3),
            Y_DN_B: (b, y + 1), OPP: (a, y + 2), MATE_OPP: (b, y + 2),
        }[what]
        right(n, what, which, yy, sib, c).wait_recv()

    def start(copies):
        for cp in copies:
            cp.start()

    def on_far(n, c):
        wait(n, FAR, c)
        start([mate_a(n, c)] + y_copies(n, 0, c))

    def on_mate(n, c):
        wait(n, MATE, c)
        start(y_copies(n, 1, c))

    def on_side(n, c):
        wait(n, Y_UP_A if n == 0 else Y_DN_A, c)
        opp_y(n, c).start()

    def on_opp(n, c):
        wait(n, OPP, c)
        start([opp_far(n, c), opp_mate(n, c)])

    def on_opp_far(n, c):
        wait(n, OPP, c)
        opp_mate(n, c).start()

    def cross(c):
        if c == 0:
            return copy(rown.at[pl.ds(*HALVES[0]), :], rb.at[1, odd, y, pl.ds(*HALVES[0]), :], CROSS, anti)
        return copy(relay, rb.at[1, 1 - odd, y, pl.ds(*HALVES[1]), :], CROSS + 1, anti)

    to_relay = copy(rown.at[pl.ds(*HALVES[1]), :], relay, RELAY, far)

    def on_cross(c):
        cross(c).wait_recv()
        start([far_a(1, c), mate_a(1, c)] + y_copies(1, 0, c))

    def prepare():
        loads[8].wait()
        for cp in range(16):
            w2[:, cp * 32 : cp * 32 + 32] = jnp.concatenate(
                [readout[cp * 64 : cp * 64 + 32, :].T, readout[cp * 64 + 32 : cp * 64 + 64, :].T], axis=0
            )
        repack(lown, z)

    @pl.when(source)
    def _():
        rb[0, odd, y] = rown[...]
        for c in range(2):
            start([far_a(0, c), mate_a(0, c)] + y_copies(0, 0, c))
            start([ring(1, z, up, c) for up in (True, False)])
        prepare()
        to_relay.wait_recv()
        cross(1).start()
        for c in range(2):
            on_mate(0, c)
            on_side(0, c)
            ring_on(1, c)
        on_cross(0)
        on_opp(0, 0)
        ring_on(2, 0)
        ring_repack(1)
        on_far(1, 1)
        ring_on(2, 1)
        on_opp(0, 1)
        on_mate(1, 0)
        on_side(1, 0)
        ring_on(3, 0)
        on_mate(1, 1)
        on_side(1, 1)
        ring_repack(2)
        ring_on(3, 1)
        ring_repack(3)

    @pl.when(jnp.logical_not(source))
    def _():
        to_relay.start()
        start([ring(1, z, up, 0) for up in (True, False)])
        cross(0).start()
        start([ring(1, z, up, 1) for up in (True, False)])
        prepare()
        for c in range(2):
            on_far(0, c)
            ring_on(1, c)
        on_mate(0, 0)
        on_cross(1)
        on_mate(0, 1)
        ring_on(2, 0)
        on_far(1, 0)
        ring_repack(1)
        ring_on(2, 1)
        on_opp_far(0, 0)
        on_opp_far(0, 1)
        on_mate(1, 0)
        ring_on(3, 0)
        ring_repack(2)
        on_mate(1, 1)
        ring_on(3, 1)
        ring_repack(3)

    for up, c in ring_pieces(4):
        ring(4, (z + 4) % 8, up, c).wait_recv()
    repack(lp.at[(z + 4) % 8], (z + 4) % 8)

    low = lax.broadcasted_iota(jnp.int32, (128, 128), 1) < 64

    def counts(s, yy):
        for which in range(2):
            t = jnp.zeros((16, 128), F32)
            for part in range(2):
                two = jnp.concatenate([lf[part], lf[part]], axis=0)
                t += lax.dot_general(
                    rb[part, which, yy, 384:400, :], two, NT, preferred_element_type=F32
                )
            cnt[s, which] = t

    def multiply(which, yy, slot):
        def tile(n, carry):
            o = None
            for part in range(2):
                lt = lc[part, pl.ds(n * 4, 4), :, :].reshape(256, 256)
                t = lax.dot_general(rb[part, which, yy, 0:384, :], lt, NT, preferred_element_type=F32)
                o = t if o is None else o + t
            ob = o.astype(BF).reshape(6, 2, 32, 256)
            for jj in range(2):
                for cl in range(2):
                    rows = pl.ds(pl.multiple_of(n * 64 + cl * 32, 32), 32)
                    xs[slot, :, rows, jj * 128 : jj * 128 + 128] = ob[:, jj, :, cl * 128 : cl * 128 + 128]
            return carry

        lax.fori_loop(0, 8, tile, 0, unroll=True)

    def project(dst, slot):
        def pair(jp, carry):
            q = jnp.dot(w2[...], xs[slot, jp], preferred_element_type=F32)
            for jj in range(2):
                j = 2 * jp + jj
                c = jnp.where(low, q[:128, jj * 128 : jj * 128 + 128], q[128:, jj * 128 : jj * 128 + 128])
                t = (c * rcs[pl.ds(j, 1), :]).T
                s = t[:64] + t[64:]
                for zi in range(4):
                    dst[pl.ds(zi * 144 + j, 12, stride=12), :] = s[zi * 16 : zi * 16 + 12]
            return carry

        lax.fori_loop(0, 6, pair, 0, unroll=True)

    def arrive(off):
        for c in range(2):
            for n in range(2):
                if off == 2:
                    wait(n, MATE_OPP, c)
                if off in (1, 3):
                    first, second = (Y_UP_A, Y_UP_B) if off == 3 else (Y_DN_A, Y_DN_B)
                    if n == (0 if off == 3 else 1):

                        @pl.when(jnp.logical_not(source))
                        def _():
                            wait(n, first, c)
                    else:
                        wait(n, first, c)
                    wait(n, second, c)

    def late(c, follow):
        @pl.when(jnp.logical_not(source) if follow else source)
        def _():
            on_opp_far(1, c) if follow else on_opp(1, c)

    def finish(s, off):
        yy = (y + off) % 4
        for d in range(3):
            zi = (zl + d + 1) % 4
            src = (zl + 3 - d) % 4
            copy(obuf.at[s, zi], orecv.at[src, yy], OUT + 3 * s + d, line[d]).wait_recv()
        got = [orecv[q, yy].astype(F32) for q in range(4)]
        at = pl.ds(pl.multiple_of(yy * 48, 16), 48)
        for i in range(12):
            new = jnp.concatenate([g[i * 12 : i * 12 + 12] for g in got], axis=0)
            out[i, at, :] = (pairs[i, at, :].astype(F32) + new).astype(BF)

    for s, off in enumerate(STEPS):
        yy = (y + off) % 4
        arrive(off)
        swap = copy(send_core.at[s], got_core.at[s], CORE + s, sib)
        counts(s, yy)
        swap_counts = copy(cnt.at[s], got_cnt.at[s], COUNT + s, sib)
        swap_counts.start()
        multiply(1 - k, yy, 0)
        if off == 0:
            late(0, False)
            multiply(k, yy, 1)
            late(1, False)
        swap_counts.wait()
        rcs[...] = 1.0 / (0.001 + cnt[s, 1 - k] + got_cnt[s, 1 - k])
        project(send_core.at[s], 0)
        swap.start()
        rcs[...] = 1.0 / (0.001 + cnt[s, k] + got_cnt[s, k])
        if off == 0:
            late(0, True)
        else:
            multiply(k, yy, 1)
            if s == 1:
                late(1, True)
        project(stage, 1)
        swap.wait_recv()
        obuf[s] = (stage[...] + got_core[s]).astype(BF).reshape(4, 144, 128)
        for d in range(3):
            zi = (zl + d + 1) % 4
            copy(obuf.at[s, zi], orecv.at[zl, yy], OUT + 3 * s + d, line[d]).start()
        orecv[zl, yy] = obuf[s, zl]
        if s == 0:
            loads[9].wait()
        else:
            finish(s - 1, STEPS[s - 1])

    finish(3, STEPS[3])

    for s in range(4):
        for d in range(3):
            zi = (zl + d + 1) % 4
            copy(obuf.at[s, zi], orecv.at[zl, y], OUT + 3 * s + d, line[d]).wait_send()
        copy(send_core.at[s], got_core.at[s], CORE + s, sib).wait_send()
    for step in range(1, 5):
        for up, c in ring_pieces(step):
            ring(step, ring_from(step - 1, up), up, c).wait_send()
    for c in range(2):
        for n in range(2):
            for cp in [mate_a(n, c), opp_mate(n, c)] + y_copies(n, 0, c) + y_copies(n, 1, c):
                cp.wait_send()

    @pl.when(source)
    def _():
        for c in range(2):
            for n in range(2):
                for cp in [opp_y(n, c), opp_far(n, c)] + ([] if (n, c) == (1, 1) else [far_a(n, c)]):
                    cp.wait_send()
        cross(1).wait_send()

    @pl.when(jnp.logical_not(source))
    def _():
        cross(0).wait_send()
        to_relay.wait_send()
        far_a(1, 1).wait_send()


def exchange(*args):
    vm = pl.BlockSpec(memory_space=pltpu.VMEM)
    return pl.pallas_call(
        kernel,
        out_shape=jax.ShapeDtypeStruct((12, 192, 128), BF),
        in_specs=[pl.BlockSpec(memory_space=pltpu.HBM)] * len(args),
        out_specs=vm,
        scratch_shapes=[
            pltpu.VMEM((BLOCK, 256), BF),
            pltpu.VMEM((BLOCK, 256), BF),
            pltpu.VMEM((8, BLOCK, 256), BF),
            pltpu.VMEM((2, 32, 64, 256), BF),
            pltpu.VMEM((2, 64, 256), BF),
            pltpu.VMEM((2, 512, 128), F32),
            pltpu.VMEM((2, 2, 4, BLOCK, 256), BF),
            pltpu.VMEM((256, 512), BF),
            pltpu.VMEM((2, 6, 512, 256), BF),
            pltpu.VMEM((4, 2, 16, 128), F32),
            pltpu.VMEM((4, 2, 16, 128), F32),
            pltpu.VMEM((16, 128), F32),
            pltpu.VMEM((576, 128), F32),
            pltpu.VMEM((4, 576, 128), F32),
            pltpu.VMEM((4, 576, 128), F32),
            pltpu.VMEM((4, 4, 144, 128), BF),
            pltpu.VMEM((4, 4, 144, 128), BF),
            pltpu.VMEM((64, 64), BF),
            pltpu.VMEM((12, 192, 128), BF),
            pltpu.VMEM((HALVES[1][1], 256), BF),
            *[pltpu.VMEM(v.shape, v.dtype) for v in args[:9]],
            pltpu.SemaphoreType.DMA((N_SEMS,)),
            pltpu.SemaphoreType.DMA((N_SEMS,)),
            pltpu.SemaphoreType.DMA((10,)),
        ],
        compiler_params=pltpu.CompilerParams(
            collective_id=0, has_side_effects=True, vmem_limit_bytes=63 * 2**20
        ),
        name="outer_mean",
    )(*args)


def body(msa, flags, scale, shift, w_left, b_left, w_right, b_right, readout, pair):
    return exchange(
        msa.transpose(1, 2, 0), flags.T, scale[None], shift[None], w_left.T, b_left[None], w_right.T, b_right[None],
        readout, pair,
    )


def solution(mesh):
    in_specs = (
        P("seq", "res", None),
        P("seq", "res"),
        P(),
        P(),
        P(),
        P(),
        P(),
        P(),
        P(),
        P("res", "seq", None),
    )
    return jax.shard_map(
        body, mesh=mesh, in_specs=in_specs, out_specs=P("res", "seq", None), check_vma=False
    )
```

time: 68.2 us -> 60.8 us (0.89)
  other arithmetic: 3.11 us -> 0 us
  local copies, waits for them, and re-layouts: 4.24 us -> 1.92 us
  Pallas kernels: 60.5 us -> 58.6 us
    pallas_call x1, Pallas kernels: 60.5 us -> 58.6 us  [exchange(): pl.pallas_call(kernel, out_shape=jax.ShapeDtypeStruct((12, 192, 128), BF)...]
    unnamed x8 -> x1, local copies, waits for them, and re-layouts: 3.61 us -> 1.92 us
    another operation x2 -> x0, other arithmetic: 1.43 us -> none  [body(): vecs = jnp.stack([scale, shift, jnp.concatenate([b_left, b_right])], axis=1)]
    convert_element_type x1 -> x0, other arithmetic: 0.96 us -> none  [body(): return (pair.astype(F32) + update.astype(F32)).astype(BF)]
    concatenate x1 -> x0, other arithmetic: 0.72 us -> none  [body(): w12 = jnp.concatenate([w_left.T, w_right.T], axis=0)]
where the time goes in v3:
time: 60.8 us; the launch traced here: 60.5 us
  Pallas kernels  58.6 us (96%)
  local copies, waits for them, and re-layouts  1.92 us (3%)
    pallas_call x1, Pallas kernels, exchange(): pl.pallas_call(kernel, out_shape=jax.ShapeDtypeStruct((12, 192, 128), BF)...  58.6 us
    unnamed x1, local copies, waits for them, and re-layouts  1.92 us

profile of v3, /device:TPU:6, one launch (start us, length us, event | category | flops | bytes accessed | tf_op | source)
XLA Modules:
  0.0 60.5 jit_solution(9521185140996035478)
XLA Ops:
  0.0 58.6 %outer_mean.1 = bf16[12,192,128]{2,1,0:T(8,128)(2,1)} custom-call(bf16[12,64,256]{2,1,0:T(8,128)(2,1)} %bitcast.8, s32[12,256]{1,0:T(8,128)} %bitcast.9, f32[1,64]{1,0:T(1,128)} %bitcast.12, f32[1,64]{1,0:T(1,128)} %bitcast.13, bf16[32,64]{1,0:T(8,128)(2,1)} %bitcast.10, f32[1,32]{1,0:T(1,128)} %bitcast.14, bf16[32,64]{1,0:T(8,128)(2,1)} %bitcast.11, ...), custom_call_target="tpu_custom_call" | custom-call | tf_op jit(solution)/shard_map/outer_mean/pallas_call | solution.py:416
  58.6 1.9 %copy.12 = bf16[12,192,128]{2,1,0:T(8,128)(2,1)} copy(bf16[12,192,128]{2,1,0:T(8,128)(2,1)} %outer_mean.1) | data formatting | bytes 1179648

commit v4 on v3

--- a/solution.py
+++ b/solution.py
@@ -267,8 +267,14 @@
         ring_on(3, 1)
         ring_repack(3)
 
+    def late(c, follow):
+        @pl.when(jnp.logical_not(source) if follow else source)
+        def _():
+            on_opp_far(1, c) if follow else on_opp(1, c)
+
     for up, c in ring_pieces(4):
         ring(4, (z + 4) % 8, up, c).wait_recv()
+    late(0, False)
     repack(lp.at[(z + 4) % 8], (z + 4) % 8)
 
     low = lax.broadcasted_iota(jnp.int32, (128, 128), 1) < 64
@@ -283,35 +289,33 @@
                 )
             cnt[s, which] = t
 
-    def multiply(which, yy, slot):
-        def tile(n, carry):
-            o = None
-            for part in range(2):
-                lt = lc[part, pl.ds(n * 4, 4), :, :].reshape(256, 256)
-                t = lax.dot_general(rb[part, which, yy, 0:384, :], lt, NT, preferred_element_type=F32)
-                o = t if o is None else o + t
-            ob = o.astype(BF).reshape(6, 2, 32, 256)
-            for jj in range(2):
-                for cl in range(2):
-                    rows = pl.ds(pl.multiple_of(n * 64 + cl * 32, 32), 32)
-                    xs[slot, :, rows, jj * 128 : jj * 128 + 128] = ob[:, jj, :, cl * 128 : cl * 128 + 128]
-            return carry
-
-        lax.fori_loop(0, 8, tile, 0, unroll=True)
-
-    def project(dst, slot):
-        def pair(jp, carry):
-            q = jnp.dot(w2[...], xs[slot, jp], preferred_element_type=F32)
-            for jj in range(2):
-                j = 2 * jp + jj
-                c = jnp.where(low, q[:128, jj * 128 : jj * 128 + 128], q[128:, jj * 128 : jj * 128 + 128])
-                t = (c * rcs[pl.ds(j, 1), :]).T
-                s = t[:64] + t[64:]
-                for zi in range(4):
-                    dst[pl.ds(zi * 144 + j, 12, stride=12), :] = s[zi * 16 : zi * 16 + 12]
-            return carry
-
-        lax.fori_loop(0, 6, pair, 0, unroll=True)
+    def sides(yy):
+        return [
+            jnp.concatenate([rb[part, 0, yy, 0:384, :], rb[part, 1, yy, 0:384, :]], axis=0)
+            for part in range(2)
+        ]
+
+    def tile(both, n):
+        o = None
+        for part in range(2):
+            lt = lc[part, pl.ds(n * 4, 4), :, :].reshape(256, 256)
+            t = lax.dot_general(both[part], lt, NT, preferred_element_type=F32)
+            o = t if o is None else o + t
+        ob = o.astype(BF).reshape(2, 6, 2, 32, 256)
+        for jj in range(2):
+            for cl in range(2):
+                rows = pl.ds(pl.multiple_of(n * 64 + cl * 32, 32), 32)
+                xs[:, :, rows, jj * 128 : jj * 128 + 128] = ob[:, :, jj, :, cl * 128 : cl * 128 + 128]
+
+    def pair(which, jp, dst, side):
+        q = jnp.dot(w2[...], xs[which, jp], preferred_element_type=F32)
+        for jj in range(2):
+            j = 2 * jp + jj
+            c = jnp.where(low, q[:128, jj * 128 : jj * 128 + 128], q[128:, jj * 128 : jj * 128 + 128])
+            t = (c * rcs[side, pl.ds(j, 1), :]).T
+            s = t[:64] + t[64:]
+            for zi in range(4):
+                dst[pl.ds(zi * 144 + j, 12, stride=12), :] = s[zi * 16 : zi * 16 + 12]
 
     def arrive(off):
         for c in range(2):
@@ -328,11 +332,6 @@
                     else:
                         wait(n, first, c)
                     wait(n, second, c)
-
-    def late(c, follow):
-        @pl.when(jnp.logical_not(source) if follow else source)
-        def _():
-            on_opp_far(1, c) if follow else on_opp(1, c)
 
     def finish(s, off):
         yy = (y + off) % 4
@@ -346,48 +345,76 @@
             new = jnp.concatenate([g[i * 12 : i * 12 + 12] for g in got], axis=0)
             out[i, at, :] = (pairs[i, at, :].astype(F32) + new).astype(BF)
 
-    for s, off in enumerate(STEPS):
-        yy = (y + off) % 4
-        arrive(off)
-        swap = copy(send_core.at[s], got_core.at[s], CORE + s, sib)
-        counts(s, yy)
-        swap_counts = copy(cnt.at[s], got_cnt.at[s], COUNT + s, sib)
-        swap_counts.start()
-        multiply(1 - k, yy, 0)
-        if off == 0:
-            late(0, False)
-            multiply(k, yy, 1)
-            late(1, False)
-        swap_counts.wait()
-        rcs[...] = 1.0 / (0.001 + cnt[s, 1 - k] + got_cnt[s, 1 - k])
-        project(send_core.at[s], 0)
-        swap.start()
-        rcs[...] = 1.0 / (0.001 + cnt[s, k] + got_cnt[s, k])
-        if off == 0:
-            late(0, True)
-        else:
-            multiply(k, yy, 1)
-            if s == 1:
-                late(1, True)
-        project(stage, 1)
-        swap.wait_recv()
+    def swap(s):
+        return copy(send_core.at[s], got_core.at[s], CORE + s, sib)
+
+    def settle(s):
+        yy = (y + STEPS[s]) % 4
+        swap(s).wait_recv()
         obuf[s] = (stage[...] + got_core[s]).astype(BF).reshape(4, 144, 128)
         for d in range(3):
             zi = (zl + d + 1) % 4
             copy(obuf.at[s, zi], orecv.at[zl, yy], OUT + 3 * s + d, line[d]).start()
         orecv[zl, yy] = obuf[s, zl]
+
+    def swap_counts(s):
+        return copy(cnt.at[s], got_cnt.at[s], COUNT + s, sib)
+
+    def begin(s):
+        arrive(STEPS[s])
+        counts(s, (y + STEPS[s]) % 4)
+        swap_counts(s).start()
+
+    def multiply(s):
+        both = sides((y + STEPS[s]) % 4)
+
+        def one(n, carry):
+            tile(both, n)
+            return carry
+
+        lax.fori_loop(0, 8, one, 0, unroll=True)
+
+    def project(s):
+        swap_counts(s).wait()
+        for side, which in ((0, 1 - k), (1, k)):
+            rcs[side] = 1.0 / (0.001 + cnt[s, which] + got_cnt[s, which])
+
+        def block(which, dst, side):
+            def one(jp, carry):
+                pair(which, jp, dst, side)
+                return carry
+
+            lax.fori_loop(0, 6, one, 0, unroll=True)
+
+        block(1 - k, send_core.at[s], 0)
+        swap(s).start()
+        block(k, stage, 1)
+
+    begin(0)
+    for s in range(4):
+        multiply(s)
         if s == 0:
+            late(1, False)
+        if s == 1:
+            late(1, True)
+        project(s)
+        if s == 0:
+            late(0, True)
+        if s < 3:
+            begin(s + 1)
+        else:
             loads[9].wait()
-        else:
-            finish(s - 1, STEPS[s - 1])
-
+            finish(0, STEPS[0])
+            finish(1, STEPS[1])
+        settle(s)
+    finish(2, STEPS[2])
     finish(3, STEPS[3])
 
     for s in range(4):
         for d in range(3):
             zi = (zl + d + 1) % 4
             copy(obuf.at[s, zi], orecv.at[zl, y], OUT + 3 * s + d, line[d]).wait_send()
-        copy(send_core.at[s], got_core.at[s], CORE + s, sib).wait_send()
+        swap(s).wait_send()
     for step in range(1, 5):
         for up, c in ring_pieces(step):
             ring(step, ring_from(step - 1, up), up, c).wait_send()
@@ -430,7 +457,7 @@
             pltpu.VMEM((2, 6, 512, 256), BF),
             pltpu.VMEM((4, 2, 16, 128), F32),
             pltpu.VMEM((4, 2, 16, 128), F32),
-            pltpu.VMEM((16, 128), F32),
+            pltpu.VMEM((2, 16, 128), F32),
             pltpu.VMEM((576, 128), F32),
             pltpu.VMEM((4, 576, 128), F32),
             pltpu.VMEM((4, 576, 128), F32),
@@ -445,17 +472,18 @@
             pltpu.SemaphoreType.DMA((10,)),
         ],
         compiler_params=pltpu.CompilerParams(
-            collective_id=0, has_side_effects=True, vmem_limit_bytes=63 * 2**20
+            collective_id=0, has_side_effects=True, vmem_limit_bytes=50_000_000
         ),
         name="outer_mean",
     )(*args)
 
 
 def body(msa, flags, scale, shift, w_left, b_left, w_right, b_right, readout, pair):
-    return exchange(
+    args = (
         msa.transpose(1, 2, 0), flags.T, scale[None], shift[None], w_left.T, b_left[None], w_right.T, b_right[None],
         readout, pair,
     )
+    return exchange(*[pltpu.with_memory_space_constraint(v, pltpu.HBM) for v in args])
 
 
 def solution(mesh):

time: 60.8 us -> 57.3 us (0.942)
  Pallas kernels: 58.6 us -> 56 us
  local copies, waits for them, and re-layouts: 1.92 us -> 0.82 us
    pallas_call x1, Pallas kernels: 58.6 us -> 56 us  [exchange(): pl.pallas_call(kernel, out_shape=jax.ShapeDtypeStruct((12, 192, 128), BF)...]
    unnamed x1, local copies, waits for them, and re-layouts: 1.92 us -> 0.82 us
where the time goes in v4:
time: 57.3 us; the launch traced here: 56.9 us
  Pallas kernels  56 us (98%)
  local copies, waits for them, and re-layouts  0.82 us (1%)
    pallas_call x1, Pallas kernels, exchange(): pl.pallas_call(kernel, out_shape=jax.ShapeDtypeStruct((12, 192, 128), BF)...  56 us

profile of v4, /device:TPU:6, one launch (start us, length us, event | category | flops | bytes accessed | tf_op | source)
XLA Modules:
  0.0 56.9 jit_solution(13438077785337711569)
XLA Ops:
  0.0 56.0 %outer_mean.1 = bf16[12,192,128]{2,1,0:T(8,128)(2,1)S(1)} custom-call(bf16[12,64,256]{2,1,0:T(8,128)(2,1)} %bitcast.8, s32[12,256]{1,0:T(8,128)} %bitcast.9, f32[1,64]{1,0:T(1,128)} %bitcast.12, f32[1,64]{1,0:T(1,128)} %bitcast.13, bf16[32,64]{1,0:T(8,128)(2,1)} %bitcast.10, f32[1,32]{1,0:T(1,128)} %bitcast.14, bf16[32,64]{1,0:T(8,128)(2,1)} %bitcast.11, ...), custom_call_target="tpu_custom_call" | custom-call | tf_op jit(solution)/shard_map/outer_mean/pallas_call | solution.py:443
  56.0 0.8 %copy.12 = bf16[12,192,128]{2,1,0:T(8,128)(2,1)} copy(bf16[12,192,128]{2,1,0:T(8,128)(2,1)S(1)} %outer_mean.1) | data formatting | bytes 1179648

commit v5 on v4

--- a/solution.py
+++ b/solution.py
@@ -17,6 +17,7 @@
 RELAY = 68
 N_SEMS = 69
 STEPS = (0, 3, 1, 2)
+AHEAD = 2
 BLOCK = 400
 HALVES = ((0, 208), (208, 192))
 
@@ -27,7 +28,7 @@
 
 def kernel(
     msa_in, flags_in, scale_in, shift_in, w_left_in, b_left_in, w_right_in, b_right_in, readout_in, pair, out,
-    lown, rown, lp, lc, lf, wide, rb, w2, xs, cnt, got_cnt, rcs, stage, send_core, got_core, obuf, orecv,
+    lown, rown, lp, lc, lf, wide, rb, w2, xs, acc, cnt, got_cnt, rcs, stage, send_core, got_core, obuf, orecv,
     w12, pairs, relay, msa, flags, scale, shift, w_left, b_left, w_right, b_right, readout, ssem, rsem, lsem,
 ):
     seq, res = lax.axis_index("seq"), lax.axis_index("res")
@@ -272,10 +273,6 @@
         def _():
             on_opp_far(1, c) if follow else on_opp(1, c)
 
-    for up, c in ring_pieces(4):
-        ring(4, (z + 4) % 8, up, c).wait_recv()
-    late(0, False)
-    repack(lp.at[(z + 4) % 8], (z + 4) % 8)
 
     low = lax.broadcasted_iota(jnp.int32, (128, 128), 1) < 64
 
@@ -289,49 +286,86 @@
                 )
             cnt[s, which] = t
 
-    def sides(yy):
-        return [
-            jnp.concatenate([rb[part, 0, yy, 0:384, :], rb[part, 1, yy, 0:384, :]], axis=0)
-            for part in range(2)
-        ]
-
-    def tile(both, n):
-        o = None
-        for part in range(2):
-            lt = lc[part, pl.ds(n * 4, 4), :, :].reshape(256, 256)
-            t = lax.dot_general(both[part], lt, NT, preferred_element_type=F32)
-            o = t if o is None else o + t
-        ob = o.astype(BF).reshape(2, 6, 2, 32, 256)
+    def sides(part, yy):
+        return jnp.concatenate([rb[part, 0, yy, 0:384, :], rb[part, 1, yy, 0:384, :]], axis=0)
+
+    def dot(side, part, n):
+        lt = lc[part, pl.ds(n * 4, 4), :, :].reshape(256, 256)
+        return lax.dot_general(side, lt, NT, preferred_element_type=F32)
+
+    def keep(o, n, cols, s):
+        ob = o.astype(BF).reshape(-1, 6, 2, 32, 256)
         for jj in range(2):
             for cl in range(2):
                 rows = pl.ds(pl.multiple_of(n * 64 + cl * 32, 32), 32)
-                xs[:, :, rows, jj * 128 : jj * 128 + 128] = ob[:, :, jj, :, cl * 128 : cl * 128 + 128]
-
-    def pair(which, jp, dst, side):
-        q = jnp.dot(w2[...], xs[which, jp], preferred_element_type=F32)
+                xs[s % 2, cols, :, rows, jj * 128 : jj * 128 + 128] = ob[:, :, jj, :, cl * 128 : cl * 128 + 128]
+
+    def loop(lo, hi, one):
+        def step(n, carry):
+            one(n)
+            return carry
+
+        lax.fori_loop(lo, hi, step, 0, unroll=True)
+
+    def ahead(s):
+        side = sides(0, (y + STEPS[s]) % 4)
+
+        def one(n):
+            acc[s, n] = dot(side, 0, n)
+
+        loop(0, 8, one)
+
+    def multiply(s, lo, hi):
+        yy = (y + STEPS[s]) % 4
+        other = sides(1, yy)
+        if s < AHEAD:
+
+            def one(n):
+                keep(acc[s, n] + dot(other, 1, n), n, slice(0, 2), s)
+        else:
+            own = sides(0, yy)
+
+            def one(n):
+                keep(dot(own, 0, n) + dot(other, 1, n), n, slice(0, 2), s)
+
+        loop(lo, hi, one)
+
+    def multiply_one(s, which, lo, hi):
+        yy = (y + STEPS[s]) % 4
+        own, other = rb[0, which, yy, 0:384, :], rb[1, which, yy, 0:384, :]
+
+        def one(n):
+            keep(dot(own, 0, n) + dot(other, 1, n), n, pl.ds(which, 1), s)
+
+        loop(lo, hi, one)
+
+    def pair(which, jp, dst, side, s):
+        q = jnp.dot(w2[...], xs[s % 2, which, jp], preferred_element_type=F32)
         for jj in range(2):
             j = 2 * jp + jj
             c = jnp.where(low, q[:128, jj * 128 : jj * 128 + 128], q[128:, jj * 128 : jj * 128 + 128])
             t = (c * rcs[side, pl.ds(j, 1), :]).T
-            s = t[:64] + t[64:]
+            u = t[:64] + t[64:]
             for zi in range(4):
-                dst[pl.ds(zi * 144 + j, 12, stride=12), :] = s[zi * 16 : zi * 16 + 12]
+                dst[pl.ds(zi * 144 + j, 12, stride=12), :] = u[zi * 16 : zi * 16 + 12]
 
     def arrive(off):
         for c in range(2):
             for n in range(2):
                 if off == 2:
                     wait(n, MATE_OPP, c)
-                if off in (1, 3):
-                    first, second = (Y_UP_A, Y_UP_B) if off == 3 else (Y_DN_A, Y_DN_B)
-                    if n == (0 if off == 3 else 1):
+                if off == 3 and n == 1:
+                    wait(1, Y_UP_A, c)
+                    wait(1, Y_UP_B, c)
+                if off == 1:
+                    if n == 1:
 
                         @pl.when(jnp.logical_not(source))
                         def _():
-                            wait(n, first, c)
+                            wait(1, Y_DN_A, c)
                     else:
-                        wait(n, first, c)
-                    wait(n, second, c)
+                        wait(0, Y_DN_A, c)
+                    wait(n, Y_DN_B, c)
 
     def finish(s, off):
         yy = (y + off) % 4
@@ -365,48 +399,67 @@
         counts(s, (y + STEPS[s]) % 4)
         swap_counts(s).start()
 
-    def multiply(s):
-        both = sides((y + STEPS[s]) % 4)
-
-        def one(n, carry):
-            tile(both, n)
-            return carry
-
-        lax.fori_loop(0, 8, one, 0, unroll=True)
-
-    def project(s):
+    def scales(s):
         swap_counts(s).wait()
         for side, which in ((0, 1 - k), (1, k)):
             rcs[side] = 1.0 / (0.001 + cnt[s, which] + got_cnt[s, which])
 
-        def block(which, dst, side):
-            def one(jp, carry):
-                pair(which, jp, dst, side)
-                return carry
-
-            lax.fori_loop(0, 6, one, 0, unroll=True)
-
-        block(1 - k, send_core.at[s], 0)
-        swap(s).start()
-        block(k, stage, 1)
-
+    def project(s, side):
+        which, dst = ((1 - k), send_core.at[s]) if side == 0 else (k, stage)
+
+        def one(jp):
+            pair(which, jp, dst, side, s)
+
+        loop(0, 6, one)
+        if side == 0:
+            swap(s).start()
+
+    for c in range(2):
+
+        @pl.when(jnp.logical_not(source))
+        def _():
+            wait(0, Y_UP_A, c)
+
+        wait(0, Y_UP_B, c)
+    for s in range(AHEAD):
+        ahead(s)
+    for up, c in ring_pieces(4):
+        ring(4, (z + 4) % 8, up, c).wait_recv()
+    late(0, False)
+    repack(lp.at[(z + 4) % 8], (z + 4) % 8)
     begin(0)
-    for s in range(4):
-        multiply(s)
-        if s == 0:
-            late(1, False)
-        if s == 1:
-            late(1, True)
-        project(s)
-        if s == 0:
-            late(0, True)
-        if s < 3:
-            begin(s + 1)
-        else:
-            loads[9].wait()
-            finish(0, STEPS[0])
-            finish(1, STEPS[1])
-        settle(s)
+    begin(1)
+    multiply(0, 0, 8)
+    late(1, False)
+    multiply(1, 0, 8)
+    scales(0)
+    project(0, 0)
+    project(0, 1)
+    late(0, True)
+    begin(2)
+    multiply(2, 0, 2)
+    settle(0)
+    late(1, True)
+    multiply(2, 2, 8)
+    scales(1)
+    project(1, 0)
+    project(1, 1)
+    scales(2)
+    project(2, 0)
+    settle(1)
+    project(2, 1)
+    begin(3)
+    multiply_one(3, 1 - k, 0, 3)
+    settle(2)
+    multiply_one(3, 1 - k, 3, 8)
+    scales(3)
+    project(3, 0)
+    multiply_one(3, k, 0, 8)
+    project(3, 1)
+    loads[9].wait()
+    finish(0, STEPS[0])
+    finish(1, STEPS[1])
+    settle(3)
     finish(2, STEPS[2])
     finish(3, STEPS[3])
 
@@ -454,7 +507,8 @@
             pltpu.VMEM((2, 512, 128), F32),
             pltpu.VMEM((2, 2, 4, BLOCK, 256), BF),
             pltpu.VMEM((256, 512), BF),
-            pltpu.VMEM((2, 6, 512, 256), BF),
+            pltpu.VMEM((2, 2, 6, 512, 256), BF),
+            pltpu.VMEM((AHEAD, 8, 768, 256), F32),
             pltpu.VMEM((4, 2, 16, 128), F32),
             pltpu.VMEM((4, 2, 16, 128), F32),
             pltpu.VMEM((2, 16, 128), F32),

time: 57.3 us -> 56.5 us (0.986)
  Pallas kernels: 56 us -> 55.4 us
    pallas_call x1, Pallas kernels: 56 us -> 55.4 us  [exchange(): pl.pallas_call(kernel, out_shape=jax.ShapeDtypeStruct((12, 192, 128), BF)...]
where the time goes in v5:
time: 56.5 us; the launch traced here: 56.2 us
  Pallas kernels  55.4 us (98%)
  local copies, waits for them, and re-layouts  0.82 us (1%)
    pallas_call x1, Pallas kernels, exchange(): pl.pallas_call(kernel, out_shape=jax.ShapeDtypeStruct((12, 192, 128), BF)...  55.4 us

profile of v5, /device:TPU:6, one launch (start us, length us, event | category | flops | bytes accessed | tf_op | source)
XLA Modules:
  0.0 56.2 jit_solution(18217207978730217333)
XLA Ops:
  0.0 55.4 %outer_mean.1 = bf16[12,192,128]{2,1,0:T(8,128)(2,1)S(1)} custom-call(bf16[12,64,256]{2,1,0:T(8,128)(2,1)} %bitcast.8, s32[12,256]{1,0:T(8,128)} %bitcast.9, f32[1,64]{1,0:T(1,128)} %bitcast.12, f32[1,64]{1,0:T(1,128)} %bitcast.13, bf16[32,64]{1,0:T(8,128)(2,1)} %bitcast.10, f32[1,32]{1,0:T(1,128)} %bitcast.14, bf16[32,64]{1,0:T(8,128)(2,1)} %bitcast.11, ...), custom_call_target="tpu_custom_call" | custom-call | tf_op jit(solution)/shard_map/outer_mean/pallas_call | solution.py:496
  55.4 0.8 %copy.12 = bf16[12,192,128]{2,1,0:T(8,128)(2,1)} copy(bf16[12,192,128]{2,1,0:T(8,128)(2,1)S(1)} %outer_mean.1) | data formatting | bytes 1179648

commit v6 on v5

--- a/solution.py
+++ b/solution.py
@@ -227,15 +227,15 @@
             on_side(0, c)
             ring_on(1, c)
         on_cross(0)
-        on_opp(0, 0)
         ring_on(2, 0)
         ring_repack(1)
         on_far(1, 1)
         ring_on(2, 1)
-        on_opp(0, 1)
         on_mate(1, 0)
         on_side(1, 0)
         ring_on(3, 0)
+        on_opp(0, 0)
+        on_opp(0, 1)
         on_mate(1, 1)
         on_side(1, 1)
         ring_repack(2)
@@ -259,13 +259,13 @@
         on_far(1, 0)
         ring_repack(1)
         ring_on(2, 1)
-        on_opp_far(0, 0)
-        on_opp_far(0, 1)
         on_mate(1, 0)
         ring_on(3, 0)
         ring_repack(2)
         on_mate(1, 1)
         ring_on(3, 1)
+        on_opp_far(0, 0)
+        on_opp_far(0, 1)
         ring_repack(3)
 
     def late(c, follow):

time: 56.5 us -> 56.3 us (level)
  no operation moved by 1% of the time
where the time goes in v6:
time: 56.3 us; the launch traced here: 56.2 us
  Pallas kernels  55.4 us (98%)
  local copies, waits for them, and re-layouts  0.82 us (1%)
    pallas_call x1, Pallas kernels, exchange(): pl.pallas_call(kernel, out_shape=jax.ShapeDtypeStruct((12, 192, 128), BF)...  55.4 us

profile of v6, /device:TPU:6, one launch (start us, length us, event | category | flops | bytes accessed | tf_op | source)
XLA Modules:
  0.0 56.2 jit_solution(16791687126300850991)
XLA Ops:
  0.0 55.4 %outer_mean.1 = bf16[12,192,128]{2,1,0:T(8,128)(2,1)S(1)} custom-call(bf16[12,64,256]{2,1,0:T(8,128)(2,1)} %bitcast.8, s32[12,256]{1,0:T(8,128)} %bitcast.9, f32[1,64]{1,0:T(1,128)} %bitcast.12, f32[1,64]{1,0:T(1,128)} %bitcast.13, bf16[32,64]{1,0:T(8,128)(2,1)} %bitcast.10, f32[1,32]{1,0:T(1,128)} %bitcast.14, bf16[32,64]{1,0:T(8,128)(2,1)} %bitcast.11, ...), custom_call_target="tpu_custom_call" | custom-call | tf_op jit(solution)/shard_map/outer_mean/pallas_call | solution.py:496
  55.4 0.8 %copy.12 = bf16[12,192,128]{2,1,0:T(8,128)(2,1)} copy(bf16[12,192,128]{2,1,0:T(8,128)(2,1)S(1)} %outer_mean.1) | data formatting | bytes 1179648
